TPU v7x, 256 devices: a whole 4x4x8 slice. The times are simulated.
256 devices in a mesh: crops: 8 (over y, x_lo), protos: 32 (over x_hi, z, core).
Axes of the slice: x: 4 (x_hi: 2, x_lo: 2; x = x_hi * 2 + x_lo), y: 4, z: 8, core: 2. Of those that a mesh axis runs over, the one named last changes fastest.
Arguments:
- teacher_feats: bfloat16 [4096, 384], P(('crops', 'protos')), may hold values from -6 to 6
- student_feats: bfloat16 [4096, 384], P(('crops', 'protos')), may hold values from -6 to 6
- proto_weight: float32 [384, 131072], P(None, 'protos')
Outputs:
- weight_grad: float32 [384, 131072], P('crops', 'protos')
- row_loss: float32 [4096], P(('crops', 'protos'))
All inputs are finite; a program needn't handle non-finite values.
Results may differ from a plain program's by a relative error of at most 0.00066.
Values may be sent and summed in bfloat16 or wider, within the bound.
No kernel may reach another device: no remote copies, remote signals or barrier semaphores. Data moves between devices by JAX's collectives and lax.ppermute only.
A program may use at most 128 MiB of HBM per device.

v0:
```python
import jax
import jax.numpy as jnp
from jax import lax
from jax.sharding import PartitionSpec as P

PROTOS = 131072
ITERS = 3
LOSS_SCALE = 8192


def unit_rows(values):
    wide = values.astype(jnp.float32)
    return (wide * lax.rsqrt(jnp.sum(wide * wide, axis=1, keepdims=True) + 1e-06)).astype(
        jnp.bfloat16
    )


def local(teacher_feats, student_feats, proto_weight):
    teacher_all, student_all = (
        lax.all_gather(teacher_feats, "protos", axis=0, tiled=True),
        lax.all_gather(student_feats, "protos", axis=0, tiled=True),
    )
    teacher_unit = unit_rows(teacher_all)
    inverse_norm = lax.rsqrt(jnp.sum(proto_weight * proto_weight, axis=0) + 1e-06)
    column_unit = proto_weight * inverse_norm[None, :]
    proto_unit = column_unit.astype(jnp.bfloat16)
    teacher_exp = jnp.exp(
        jnp.dot(teacher_unit, proto_unit, preferred_element_type=jnp.float32) / 0.07
    )
    group_rows = teacher_exp.shape[0]
    total_rows = group_rows * lax.axis_size("crops")
    row_scale = jnp.ones((group_rows,), jnp.float32)
    col_scale = jnp.ones((teacher_exp.shape[1],), jnp.float32)
    for step in range(ITERS):
        weighted = jnp.dot(row_scale, teacher_exp, precision=lax.Precision.HIGHEST)
        col_sum = lax.psum(col_scale * weighted, "crops")
        col_scale = col_scale / (PROTOS * col_sum)
        partial_rows = jnp.dot(teacher_exp, col_scale, precision=lax.Precision.HIGHEST)
        row_sum = lax.psum(row_scale * partial_rows, "protos")
        row_scale = row_scale / (total_rows * row_sum)
    student_unit = unit_rows(student_all)
    logits = jnp.dot(student_unit, proto_unit, preferred_element_type=jnp.float32) / 0.1
    exp_total = lax.psum(jnp.sum(jnp.exp(logits), axis=1), "protos")
    log_total = jnp.log(exp_total)
    targets = total_rows * teacher_exp * row_scale[:, None] * col_scale[None, :]
    cross = lax.psum_scatter(
        jnp.sum(targets * logits, axis=1), "protos", scatter_dimension=0, tiled=True
    )
    piece = group_rows // lax.axis_size("protos")
    own_total = lax.dynamic_slice_in_dim(log_total, lax.axis_index("protos") * piece, piece, 0)
    row_loss = own_total - cross
    logit_grad = (LOSS_SCALE * (jnp.exp(logits - log_total[:, None]) - targets) / 0.1).astype(
        jnp.bfloat16
    )
    share = proto_weight.shape[0] // lax.axis_size("crops")
    begin = lax.axis_index("crops") * share
    local_grad = lax.dot_general(
        student_unit, logit_grad, (((0,), (0,)), ((), ())), preferred_element_type=jnp.float32
    )
    unit_grad = lax.psum(local_grad, "crops")
    inner = jnp.sum(column_unit * unit_grad, axis=0)
    complete = (unit_grad - column_unit * inner[None, :]) * inverse_norm[None, :]
    weight_grad = lax.dynamic_slice_in_dim(complete, begin, share, 0)
    return (weight_grad, row_loss)


def solution(mesh):
    placed = (P(("crops", "protos"), None), P(("crops", "protos"), None), P(None, "protos"))
    return jax.shard_map(
        local,
        mesh=mesh,
        in_specs=placed,
        out_specs=(P("crops", "protos"), P(("crops", "protos"))),
        check_vma=False,
    )
```

profile of v0, /device:TPU:2, one launch (start us, length us, event | category | flops | bytes accessed | tf_op | source)
XLA Modules:
  0.0 800.5 jit_solution(12451255184041418947)
XLA Ops:
  7.2 0.0 copy-start.3
  7.2 0.0 all-reduce.4.cloned.1.call-start
  7.2 0.0 copy-start.2
  7.2 3.5 multiply_reduce_fusion.2
  10.8 1.0 copy-done.2
  11.8 1.0 broadcast_multiply_fusion
  12.8 0.0 copy-done.3
  12.8 0.0 copy-start.1
  12.8 44.9 %all_gather.7 = bf16[512,384]{1,0:T(8,128)(2,1)S(1)} all-gather(bf16[16,384]{1,0:T(8,128)(2,1)S(1)} %copy-done.3), channel_id=1, replica_groups=mesh['crops'=8,'protos'=32] {'protos'}, dimensions={0}, use_global_device_ids=true | all-gather | bytes 405504 | tf_op jit(solution)/shard_map/all_gather | solution.py:20
  57.7 0.2 fusion.11
  57.8 2.5 multiply_exponential_fusion
  60.3 0.0 copy-start
  60.4 3.2 copy-done
  63.6 4.0 fusion.18
  67.6 0.0 copy-done.1
  67.6 30.7 %psum.57 = f32[4096]{0:T(1024)S(1)} all-reduce(f32[4096]{0:T(1024)S(1)} %bitcast.27), channel_id=1, replica_groups=mesh['crops'=8,'protos'=32] {'crops'}, use_global_device_ids=true, to_apply=%region_5.0 | all-reduce | flops 4096 | bytes 32768 | tf_op jit(solution)/shard_map/psum | solution.py:36
  98.3 9.4 %fusion.25 = f32[1,512]{1,0:T(1,128)S(1)} fusion(f32[512,4096]{1,0:T(8,128)} %copy-done, f32[4096,1]{0,1:T(1,128)S(1)} %bitcast.28), kind=kOutput, calls=%fused_computation.48 | convolution fusion | flops 25165824 | bytes 8407040 | tf_op jit(solution)/shard_map/dot_general | solution.py:38
  107.8 65.2 %psum.58 = f32[512]{0:T(512)S(1)} all-reduce(f32[512]{0:T(512)S(1)} %bitcast.32), channel_id=1, replica_groups=mesh['crops'=8,'protos'=32] {'protos'}, use_global_device_ids=true, to_apply=%region_6.0 | all-reduce | flops 512 | bytes 4096 | tf_op jit(solution)/shard_map/psum | solution.py:39
  173.0 6.3 fusion.26
  179.3 33.0 %psum.59 = f32[4096]{0:T(1024)S(1)} all-reduce(f32[4096]{0:T(1024)S(1)} %fusion.24), channel_id=1, replica_groups=mesh['crops'=8,'protos'=32] {'crops'}, use_global_device_ids=true, to_apply=%region_7.0 | all-reduce | flops 4096 | bytes 32768 | tf_op jit(solution)/shard_map/psum | solution.py:36
  212.3 9.4 %fusion.27 = f32[1,512]{1,0:T(1,128)S(1)} fusion(f32[512,4096]{1,0:T(8,128)} %copy-done, f32[4096,1]{0,1:T(1,128)S(1)} %bitcast.24), kind=kOutput, calls=%fused_computation.50 | convolution fusion | flops 25165824 | bytes 8407040 | tf_op jit(solution)/shard_map/dot_general | solution.py:38
  221.8 65.0 %psum.60 = f32[512]{0:T(512)S(1)} all-reduce(f32[512]{0:T(512)S(1)} %fusion.23), channel_id=1, replica_groups=mesh['crops'=8,'protos'=32] {'protos'}, use_global_device_ids=true, to_apply=%region_8.0 | all-reduce | flops 512 | bytes 4096 | tf_op jit(solution)/shard_map/psum | solution.py:39
  286.8 0.0 copy-start.4
  286.8 6.4 fusion.28
  293.2 30.8 %psum.61 = f32[4096]{0:T(1024)S(1)} all-reduce(f32[4096]{0:T(1024)S(1)} %mul.126), channel_id=1, replica_groups=mesh['crops'=8,'protos'=32] {'crops'}, use_global_device_ids=true, to_apply=%region_9.0 | all-reduce | flops 4096 | bytes 32768 | tf_op jit(solution)/shard_map/psum | solution.py:36
  324.0 9.4 %fusion.29 = f32[1,512]{1,0:T(1,128)S(1)} fusion(f32[512,4096]{1,0:T(8,128)} %copy-done, f32[4096,1]{0,1:T(1,128)S(1)} %bitcast.23), kind=kOutput, calls=%fused_computation.52 | convolution fusion | flops 25165824 | bytes 8407040 | tf_op jit(solution)/shard_map/dot_general | solution.py:38
  333.4 65.0 %psum.62 = f32[512]{0:T(512)S(1)} all-reduce(f32[512]{0:T(512)S(1)} %mul.128), channel_id=1, replica_groups=mesh['crops'=8,'protos'=32] {'protos'}, use_global_device_ids=true, to_apply=%region_10.0 | all-reduce | flops 512 | bytes 4096 | tf_op jit(solution)/shard_map/psum | solution.py:39
  398.5 0.0 copy-done.4
  398.5 37.7 %all_gather.6 = bf16[512,384]{1,0:T(8,128)(2,1)S(1)} all-gather(bf16[16,384]{1,0:T(8,128)(2,1)S(1)} %copy-done.4), channel_id=1, replica_groups=mesh['crops'=8,'protos'=32] {'protos'}, dimensions={0}, use_global_device_ids=true | all-gather | bytes 405504 | tf_op jit(solution)/shard_map/all_gather | solution.py:21
  436.2 0.2 fusion.9
  436.3 10.0 %multiply_reduce_fusion = (f32[512]{0:T(512)S(1)}, f32[512]{0:T(512)S(1)}, f32[512,4096]{1,0:T(8,128)}) fusion(f32[512,4096]{1,0:T(8,128)} %copy-done, f32[4096]{0:T(1024)S(1)} %multiply_divide_fusion, f32[512]{0:T(512)S(1)} %divide_multiply_fusion, f32[384,4096]{1,0:T(8,128)} %copy-done.1, bf16[512,384]{1,0:T(8,128)(2,1)S(1)} %all_gather.6, ...), kind=kOutput, calls=%fused_computation | convolution fusion | flops 1625357312 | bytes 23486464 | tf_op jit(solution)/shard_map/dot_general | solution.py:42
  446.4 66.9 %all-reduce.1 = (f32[512]{0:T(512)S(1)}, f32[512]{0:T(512)S(1)}) all-reduce(f32[512]{0:T(512)S(1)} %get-tuple-element.3, f32[512]{0:T(512)S(1)} %get-tuple-element.2), channel_id=1, replica_groups=mesh['crops'=8,'protos'=32] {'protos'}, use_global_device_ids=true, to_apply=%region_3.0 | all-reduce | flops 1024 | bytes 8192 | tf_op jit(solution)/shard_map/psum | solution.py:43
  513.3 0.0 copy-start.5
  513.3 11.9 %fusion = f32[384,4096]{1,0:T(8,128)} fusion(f32[512,4096]{1,0:T(8,128)} %copy-done, f32[512,4096]{1,0:T(8,128)} %get-tuple-element.6, f32[4096]{0:T(1024)S(1)} %multiply_divide_fusion, f32[512]{0:T(512)S(1)} %divide_multiply_fusion, f32[512]{0:T(512)S(1)} %log.3, bf16[512,384]{1,0:T(8,128)(2,1)S(1)} %all_gather.6, f32[512]{0:T(512)S(1)} %add_rsqrt_fusion.2), kind=kOutput, calls=%fused_computation.7 | convolution fusion | flops 1625882624 | bytes 23484416 | tf_op jit(solution)/shard_map/dot_general | solution.py:57
  525.2 0.0 all-reduce.4.cloned.1.call-update
  525.2 0.0 copy-done.5
  525.2 0.6 dynamic-slice
  526.5 0.6 dynamic-slice_subtract_fusion.1
  527.1 258.4 %all-reduce.4.cloned.1.call-done = f32[384,4096]{1,0:T(8,128)} async-done(((f32[384,4096]{1,0:T(8,128)}), f32[384,4096]{1,0:T(8,128)}) %all-reduce.4.cloned.1.call-update) | async-done | bytes 6291472 | tf_op jit(solution)/shard_map/psum | solution.py:60
  785.5 5.9 multiply_reduce_fusion.1
  791.3 2.4 fusion.13
  (14 shorter events, 0.1 us)
Async XLA Ops:
  7.2 5.6 copy-start.3
  7.2 778.3 %all-reduce.4.cloned.1.call-start = ((), (), s32[]{:S(2)}) async-start(), calls=%async_computation | async-start | bytes 12582912 | tf_op jit(solution)/shard_map/psum | solution.py:60
  7.2 4.6 copy-start.2
  12.8 54.8 %copy-start.1 = (f32[384,4096]{1,0:T(8,128)}, f32[384,4096]{1,0:T(8,128)S(1)}, u32[]{:S(2)}) copy-start(f32[384,4096]{1,0:T(8,128)S(1)} %broadcast_multiply_fusion) | copy-start | bytes 18874372
  60.3 3.2 copy-start
  286.8 111.7 %copy-start.4 = (bf16[16,384]{1,0:T(8,128)(2,1)S(1)}, bf16[16,384]{1,0:T(8,128)(2,1)}, u32[]{:S(2)}) copy-start(bf16[16,384]{1,0:T(8,128)(2,1)} %param.4) | copy-start | bytes 36868
  513.3 11.9 %copy-start.5 = (u32[256]{0:T(256)S(1)}, u32[256]{0:T(256)}, u32[]{:S(2)}) copy-start(u32[256]{0:T(256)} %constant.46) | copy-start | bytes 3076
Sparse Core Ops, SparseCore 0:
  525.3 260.1 all-reduce.3
where the time goes:
time: 802 us; the launch traced here: 801 us
  blocking collectives  439 us (55%)
  waiting for transfers between devices  258 us (32%)
  matrix products  69.4 us (9%)
  between operations  14.8 us (2%)
  other arithmetic  13.7 us (2%)
    psum x1, waiting for transfers between devices, local(): unit_grad = lax.psum(local_grad, 'crops')  258 us
    psum x3, blocking collectives, local(): row_sum = lax.psum(row_scale * partial_rows, 'protos')  195 us
    psum x3, blocking collectives, local(): col_sum = lax.psum(col_scale * weighted, 'crops')  94.5 us
    psum x1, blocking collectives, local(): exp_total = lax.psum(jnp.sum(jnp.exp(logits), axis=1), 'protos')  66.9 us
    all_gather x1, blocking collectives, local(): lax.all_gather(teacher_feats, 'protos', axis=0, tiled=True)  44.9 us
    all_gather x1, blocking collectives, local(): lax.all_gather(student_feats, 'protos', axis=0, tiled=True)  37.7 us
    dot_general x3, matrix products, local(): jnp.dot(teacher_exp, col_scale, precision=lax.Precision.HIGHEST)  28.3 us
    dot_general x3, matrix products, local(): weighted = jnp.dot(row_scale, teacher_exp, precision=lax.Precision.HIGHEST)  16.7 us
  transfers between devices with their start and end apart: 1, of which 1 were waited for; matrix products, arithmetic and copies ran while one was open for 0% of the time, Pallas kernels for 0%

commit v1 on v0

v1 whole, which is shorter than its diff:
```python
import math

import jax
import jax.numpy as jnp
from jax import lax
from jax.experimental import pallas as pl
from jax.experimental.pallas import tpu as pltpu
from jax.sharding import PartitionSpec as P

D = 384
PROTOS = 131072
CROPS = 4096
LOSS_SCALE = 8192
LANES = 128
MIB = 1 << 20
F32 = jnp.float32
BF16 = jnp.bfloat16
HIGHEST = lax.Precision.HIGHEST
TEACHER = math.log2(math.e) / 0.07
STUDENT = 1.0 / 0.1
LOG2E = math.log2(math.e)
VMEM = pl.BlockSpec(memory_space=pltpu.VMEM)
SMEM = pl.BlockSpec(memory_space=pltpu.SMEM)
HBM = pl.BlockSpec(memory_space=pltpu.HBM)


def params(mib=24):
    return pltpu.CompilerParams(vmem_limit_bytes=mib * MIB)


def pinned(x):
    return pltpu.with_memory_space_constraint(x, pltpu.VMEM)


def in_hbm(x):
    return pltpu.with_memory_space_constraint(x, pltpu.HBM)


def cost(flops=0, read=0, exps=0):
    return pl.CostEstimate(flops=int(flops), bytes_accessed=int(read), transcendentals=int(exps))


def unit(values):
    wide = values.astype(F32)
    return (wide * lax.rsqrt(jnp.sum(wide * wide, axis=1, keepdims=True) + 1e-6)).astype(BF16)


def own_kernel(teacher, student, out):
    rows = jnp.concatenate([unit(teacher[...]), unit(student[...])], axis=1)
    for k in range(out.shape[0]):
        out[k] = rows


def prep_kernel(weight, units, inverse, held, sems):
    blocks = held.shape[0]
    width = held.shape[2]
    copies = []
    for k in range(blocks):
        copy = pltpu.make_async_copy(weight.at[:, pl.ds(k * width, width)], held.at[k], sems.at[k])
        copy.start()
        copies.append(copy)
    for k in range(blocks):
        copies[k].wait()
        total = jnp.zeros((8, width), F32)
        for d in range(0, D, 8):
            part = held[k, d : d + 8, :]
            total += part * part
        inv = lax.rsqrt(jnp.sum(total, axis=0, keepdims=True) + 1e-6)
        inverse[:, k * width : (k + 1) * width] = inv
        for d in range(0, D, 16):
            units[d : d + 16, k * width : (k + 1) * width] = (held[k, d : d + 16, :] * inv).astype(BF16)


def col_rows(total, sums, start):
    for t in range(sums.shape[1] // LANES):
        total[start + t : start + t + 1, :] = sums[:, t * LANES : (t + 1) * LANES]


def exp_kernel(where, mine, other, units, table, student, out, total):
    core = where[0]
    half = mine.shape[0]
    first = pl.multiple_of(core * half, half)
    second = pl.multiple_of((1 - core) * half, half)
    student[pl.ds(first, half), :] = mine[:, D:]
    student[pl.ds(second, half), :] = other[:, D:]
    width = 512
    for k in range(table.shape[1] // width):
        cols = slice(k * width, (k + 1) * width)
        sums = jnp.zeros((8, width), F32)
        for start, rows in ((first, mine), (second, other)):
            e = jnp.exp2(
                jnp.dot(rows[:, :D], units[:, cols], preferred_element_type=F32) * TEACHER
            )
            table[pl.ds(start, half), cols] = e
            for d in range(0, half, 8):
                sums += e[d : d + 8, :]
        col_rows(total, jnp.sum(sums, axis=0, keepdims=True), k * width // LANES)
    every = total[...]
    for k in range(out.shape[0]):
        out[k] = every


def col_scales(parts, scale):
    scale[...] = 1.0 / (PROTOS * jnp.sum(parts[...], axis=0))


def lane_sums(acc):
    ones = jnp.ones((8, LANES), F32)
    sums = lax.dot_general(
        ones, acc, (((1,), (1,)), ((), ())), precision=HIGHEST, preferred_element_type=F32
    )
    return sums[0:1, :]


def row_kernel(table, parts, out, scale, acc, total):
    col_scales(parts, scale)
    rows, cols = table.shape
    step = 64
    for i in range(0, rows, step):
        sums = jnp.zeros((step, LANES), F32)
        for j in range(cols // LANES):
            sums += table[i : i + step, j * LANES : (j + 1) * LANES] * scale[j : j + 1, :]
        acc[i : i + step, :] = sums
    col_rows(total, lane_sums(acc[...]), 0)
    every = total[...]
    for k in range(out.shape[0]):
        out[k] = every


def down(vector):
    return jnp.transpose(jnp.broadcast_to(vector, (LANES, LANES)))


def col_kernel(table, parts, out, weight, total):
    rows, cols = table.shape
    scale = 1.0 / (CROPS * jnp.sum(parts[...], axis=0))
    for t in range(rows // LANES):
        weight[t * LANES : (t + 1) * LANES, :] = down(scale[t : t + 1, :])
    tiles = 8
    for j in range(0, cols, tiles * LANES):
        sums = [jnp.zeros((8, LANES), F32) for _ in range(tiles)]
        for i in range(0, rows, 8):
            w = weight[i : i + 8, :]
            for t in range(tiles):
                sums[t] += table[i : i + 8, j + t * LANES : j + (t + 1) * LANES] * w
        for t in range(tiles):
            row = j // LANES + t
            total[row : row + 1, :] = jnp.sum(sums[t], axis=0, keepdims=True)
    every = total[...]
    for k in range(out.shape[0]):
        out[k] = every


def last_kernel(table, parts, student, units, out, scale, acc, total):
    col_scales(parts, scale)
    rows, cols = table.shape
    acc[...] = jnp.zeros_like(acc)
    width = 512
    step = 256
    for k in range(0, cols, width):
        for i in range(0, rows, step):
            z = jnp.dot(
                student[i : i + step, :], units[:, k : k + width], preferred_element_type=F32
            )
            z = z * STUDENT
            x = jnp.exp2(z * LOG2E)
            plain = cross = exps = None
            for t in range(width // LANES):
                j = k // LANES + t
                here = slice(t * LANES, (t + 1) * LANES)
                e = table[i : i + step, j * LANES : (j + 1) * LANES] * scale[j : j + 1, :]
                zt, xt = z[:, here], x[:, here]
                plain = e if t == 0 else plain + e
                cross = e * zt if t == 0 else cross + e * zt
                exps = xt if t == 0 else exps + xt
            acc[0, i : i + step, :] += plain
            acc[1, i : i + step, :] += cross
            acc[2, i : i + step, :] += exps
    total[...] = jnp.zeros_like(total)
    for n in range(3):
        col_rows(total, lane_sums(acc[n]), n * rows // LANES)
    every = total[...]
    for k in range(out.shape[0]):
        out[k] = every


def loss_kernel(parts, out, loss):
    sums = jnp.sum(parts[...], axis=0)
    n = loss.shape[0]
    plain, cross, exps = (sums[k * n : (k + 1) * n, :] for k in range(3))
    loss[...] = jnp.log(exps) - cross / plain
    every = jnp.concatenate(
        [(LOSS_SCALE / 0.1) / exps, (LOSS_SCALE / 0.1) / plain], axis=0
    )
    for k in range(out.shape[0]):
        out[k] = every


def grad_kernel(
    where, mine, other, units, weight, inverse, scale, factors, out,
    held, wsub, punit, csub, grad, sems, wsem,
):
    core, place = where[0], where[1]
    groups = factors.shape[0]
    width = wsub.shape[1]
    half = mine.shape[0] // groups
    begin = pl.multiple_of(place * width, width)
    wcopy = pltpu.make_async_copy(weight.at[:, pl.ds(begin, width)], wsub, wsem)
    wcopy.start()

    def piece(g, side):
        src = (mine, other)[side]
        return pltpu.make_async_copy(
            src.at[pl.ds(g * half, half), :],
            held.at[side, pl.ds(g * half, half), :],
            sems.at[side, g],
        )

    for g in range(groups):
        for side in range(2):
            piece(g, side).start()
    punit[...] = units[:, pl.ds(begin, width)]
    inv = inverse[:, pl.ds(begin, width)]
    tiles = width // LANES
    for t in range(tiles):
        csub[:, t * LANES : (t + 1) * LANES] = scale[pl.ds(place * tiles + t, 1), :]
    grad[...] = jnp.zeros_like(grad)
    chunks = half // LANES

    def body(g, carry):
        for side in range(2):
            piece(g, side).wait()
            number = core if side == 0 else 1 - core
            rows = held[side, pl.ds(pl.multiple_of(g * half, half), half), :]
            t_rows, s_rows = rows[:, :D], rows[:, D:]
            zt = jnp.dot(t_rows, punit[...], preferred_element_type=F32)
            zs = jnp.dot(s_rows, punit[...], preferred_element_type=F32)
            a = jnp.concatenate(
                [down(factors[g, pl.ds(number * chunks + n, 1), :]) for n in range(chunks)], axis=0
            )
            b = jnp.concatenate(
                [down(factors[g, pl.ds((2 + number) * chunks + n, 1), :]) for n in range(chunks)],
                axis=0,
            )
            parts = []
            for t in range(tiles):
                here = slice(t * LANES, (t + 1) * LANES)
                e = jnp.exp2(zt[:, here] * TEACHER) * (csub[:, here] * b)
                x = jnp.exp2(zs[:, here] * (STUDENT * LOG2E)) * a
                parts.append((x - e).astype(BF16))
            logit_grad = jnp.concatenate(parts, axis=1)
            grad[...] += lax.dot_general(
                s_rows, logit_grad, (((0,), (0,)), ((), ())), preferred_element_type=F32
            )
        return carry

    lax.fori_loop(0, groups, body, 0)
    wcopy.wait()
    inner = jnp.zeros((8, width), F32)
    for d in range(0, D, 8):
        inner += wsub[d : d + 8, :] * inv * grad[d : d + 8, :]
    inner = jnp.sum(inner, axis=0, keepdims=True)
    share = out.shape[1]
    for d in range(0, D, 8):
        cu = wsub[d : d + 8, :] * inv
        out[d // share, d % share : d % share + 8, :] = (grad[d : d + 8, :] - cu * inner) * inv


def struct(shape, dtype=F32):
    return jax.ShapeDtypeStruct(shape, dtype)


def local(teacher_feats, student_feats, proto_weight):
    crops, protos = lax.axis_size("crops"), lax.axis_size("protos")
    own = teacher_feats.shape[0]
    rows = own * protos
    half = rows // 2
    cols = proto_weight.shape[1]
    width = cols // crops
    share = D // crops
    ctile, rtile = cols // LANES, rows // LANES
    number = lax.axis_index("protos")
    place = lax.axis_index("crops")
    where = jnp.stack([number % 2, place]).astype(jnp.int32)
    swap = [(j, j ^ 1) for j in range(protos)]
    same_core = [[j for j in range(protos) if j % 2 == core] for core in range(2)]

    copies = pl.pallas_call(
        own_kernel,
        out_shape=struct((protos // 2, own, 2 * D), BF16),
        in_specs=[VMEM, VMEM],
        out_specs=VMEM,
    )(teacher_feats, student_feats)
    mine = lax.all_to_all(
        copies, "protos", 0, 0, tiled=True, axis_index_groups=same_core
    ).reshape(half, 2 * D)
    other = lax.ppermute(mine, "protos", swap)
    all_mine = lax.all_gather(mine, "crops", axis=0, tiled=True)

    units, inverse = pl.pallas_call(
        prep_kernel,
        out_shape=(pltpu.VMEM((D, cols), BF16), pltpu.VMEM((1, cols), F32)),
        in_specs=[HBM],
        out_specs=(VMEM, VMEM),
        scratch_shapes=[pltpu.VMEM((8, D, cols // 8), F32), pltpu.SemaphoreType.DMA((8,))],
        compiler_params=params(),
        cost_estimate=cost(3 * D * cols, 4 * D * cols),
    )(in_hbm(proto_weight))

    table, student, parts = pl.pallas_call(
        exp_kernel,
        out_shape=(
            pltpu.VMEM((rows, cols), F32),
            pltpu.VMEM((rows, D), BF16),
            struct((crops, ctile, LANES)),
        ),
        in_specs=[SMEM, VMEM, VMEM, VMEM],
        out_specs=(VMEM, VMEM, VMEM),
        scratch_shapes=[pltpu.VMEM((ctile, LANES), F32)],
        compiler_params=params(),
        cost_estimate=cost(2 * rows * D * cols, 0, rows * cols),
    )(where, mine, other, pinned(units))

    def over_crops(x):
        return lax.all_to_all(x, "crops", 0, 0, tiled=True)

    def over_protos(x):
        return lax.all_to_all(x, "protos", 0, 0, tiled=True)

    for step in range(2):
        rparts, _ = pl.pallas_call(
            row_kernel,
            out_shape=(struct((protos, rtile, LANES)), struct((ctile, LANES))),
            in_specs=[VMEM, VMEM],
            out_specs=(VMEM, VMEM),
            scratch_shapes=[pltpu.VMEM((rows, LANES), F32), pltpu.VMEM((rtile, LANES), F32)],
            compiler_params=params(),
            cost_estimate=cost(2 * rows * cols),
        )(pinned(table), over_crops(parts))
        parts = pl.pallas_call(
            col_kernel,
            out_shape=struct((crops, ctile, LANES)),
            in_specs=[VMEM, VMEM],
            out_specs=VMEM,
            scratch_shapes=[pltpu.VMEM((rows, LANES), F32), pltpu.VMEM((ctile, LANES), F32)],
            compiler_params=params(),
            cost_estimate=cost(2 * rows * cols),
        )(pinned(table), over_protos(rparts))

    rparts, scale = pl.pallas_call(
        last_kernel,
        out_shape=(struct((protos, 4 * rtile, LANES)), struct((ctile, LANES))),
        in_specs=[VMEM, VMEM, VMEM, VMEM],
        out_specs=(VMEM, VMEM),
        scratch_shapes=[pltpu.VMEM((3, rows, LANES), F32), pltpu.VMEM((4 * rtile, LANES), F32)],
        compiler_params=params(),
        cost_estimate=cost(2 * rows * D * cols, 0, rows * cols),
    )(pinned(table), over_crops(parts), pinned(student), pinned(units))

    all_mine, rparts = lax.optimization_barrier((all_mine, rparts))
    all_other = lax.ppermute(all_mine, "protos", swap)
    factors, loss = pl.pallas_call(
        loss_kernel,
        out_shape=(struct((crops, 2 * rtile, LANES)), struct((rtile, LANES))),
        in_specs=[VMEM],
        out_specs=(VMEM, VMEM),
    )(over_protos(rparts))
    first = (number % 2) * half + (number // 2) * own
    row_loss = lax.dynamic_slice(loss.reshape(rows), (first,), (own,))

    grad = pl.pallas_call(
        grad_kernel,
        out_shape=struct((crops, share, width)),
        in_specs=[SMEM, HBM, HBM, VMEM, HBM, VMEM, VMEM, VMEM],
        out_specs=VMEM,
        scratch_shapes=[
            pltpu.VMEM((2, crops * half, 2 * D), BF16),
            pltpu.VMEM((D, width), F32),
            pltpu.VMEM((D, width), BF16),
            pltpu.VMEM((1, width), F32),
            pltpu.VMEM((D, width), F32),
            pltpu.SemaphoreType.DMA((2, crops)),
            pltpu.SemaphoreType.DMA,
        ],
        compiler_params=params(),
        cost_estimate=cost(6 * CROPS * D * width, 0, 2 * CROPS * width),
    )(
        where, in_hbm(all_mine), in_hbm(all_other), pinned(units), in_hbm(proto_weight),
        pinned(inverse), scale, over_crops(factors),
    )
    moved = lax.all_to_all(grad, "crops", 0, 0, tiled=True)
    weight_grad = moved.transpose(1, 0, 2).reshape(share, cols)
    return (weight_grad, row_loss)


def solution(mesh):
    placed = (P(("crops", "protos"), None), P(("crops", "protos"), None), P(None, "protos"))
    return jax.shard_map(
        local,
        mesh=mesh,
        in_specs=placed,
        out_specs=(P("crops", "protos"), P(("crops", "protos"))),
        check_vma=False,
    )
```

time: 802 us -> 181 us (0.23)
  blocking collectives: 439 us -> 120 us
  waiting for transfers between devices: 258 us -> 8.85 us
  matrix products: 69.4 us -> 0 us
  Pallas kernels: 0 us -> 29.2 us
  other arithmetic: 13.7 us -> 0.08 us
    psum x7 -> x0, blocking collectives: 357 us -> none  [the longest x3 195 us: local(): row_sum = lax.psum(row_scale * partial_rows, 'protos')]
    psum x1 -> x0, waiting for transfers between devices: 258 us -> none  [local(): unit_grad = lax.psum(local_grad, 'crops')]
    all_to_all x0 -> x8, blocking collectives: none -> 120 us  [the longest x3 51.1 us: over_protos(): return lax.all_to_all(x, 'protos', 0, 0, tiled=True)]
    all_gather x2 -> x0, blocking collectives: 82.5 us -> none  [the longest x1 44.9 us: local(): lax.all_gather(teacher_feats, 'protos', axis=0, tiled=True)]
    dot_general x9 -> x0, matrix products: 69.4 us -> none  [the longest x3 28.3 us: local(): jnp.dot(teacher_exp, col_scale, precision=lax.Precision.HIGHEST)]
    pallas_call x0 -> x10, Pallas kernels: none -> 29.2 us  [the longest x1 12.2 us: local(): pl.pallas_call(grad_kernel, out_shape=struct((crops, share, width)), in_s...]
    reduce_sum x4 -> x0, other arithmetic: 9.69 us -> none  [the longest x1 5.86 us: local(): inner = jnp.sum(column_unit * unit_grad, axis=0)]
    all_to_all x0 -> x1, waiting for transfers between devices: none -> 8.81 us  [local(): moved = lax.all_to_all(grad, 'crops', 0, 0, tiled=True)]
  transfers between devices with their start and end apart: 1 -> 4, of which waited for: 1 -> 1; matrix products, arithmetic and copies ran while one was open for 0% -> 1% of each run, Pallas kernels for 0% -> 9%
where the time goes in v1:
time: 181 us; the launch traced here: 180 us
  blocking collectives  120 us (66%)
  Pallas kernels  29.2 us (16%)
  between operations  14.1 us (8%)
  waiting for transfers between devices  8.85 us (5%)
  starting transfers between devices  5.22 us (3%)
  local copies, waits for them, and re-layouts  3.08 us (2%)
    all_to_all x3, blocking collectives, over_protos(): return lax.all_to_all(x, 'protos', 0, 0, tiled=True)  51.1 us
    all_to_all x4, blocking collectives, over_crops(): return lax.all_to_all(x, 'crops', 0, 0, tiled=True)  44.4 us
    all_to_all x1, blocking collectives, local(): lax.all_to_all(copies, 'protos', 0, 0, tiled=True, axis_index_groups=same...  24.4 us
    pallas_call x1, Pallas kernels, local(): pl.pallas_call(grad_kernel, out_shape=struct((crops, share, width)), in_s...  12.2 us
    all_to_all x1, waiting for transfers between devices, local(): moved = lax.all_to_all(grad, 'crops', 0, 0, tiled=True)  8.81 us
    all_to_all x1, starting transfers between devices, local(): moved = lax.all_to_all(grad, 'crops', 0, 0, tiled=True)  4.82 us
    pallas_call x1, Pallas kernels, local(): pl.pallas_call(last_kernel, out_shape=(struct((protos, 4 * rtile, LANES))...  3.88 us
  transfers between devices with their start and end apart: 4, of which 1 were waited for; matrix products, arithmetic and copies ran while one was open for 1% of the time, Pallas kernels for 9%

profile of v1, /device:TPU:2, one launch (start us, length us, event | category | flops | bytes accessed | tf_op | source)
XLA Modules:
  0.0 180.3 jit_solution(15983768816397879804)
XLA Ops:
  7.2 0.0 all-gather.2.cloned.1.call-start
  7.2 1.6 shard_map.50
  8.8 24.4 %all_to_all.45 = bf16[16,16,768]{2,1,0:T(8,128)(2,1)} all-to-all(bf16[16,16,768]{2,1,0:T(8,128)(2,1)} %shard_map.50), channel_id=1, replica_groups={{0,2,4,6,8,10,12,14,16,18,20,22,24,26,28,30},{1,3,5,7,9,11,13,15,17,19,..., dimensions={0} | all-to-all | bytes 786432 | tf_op jit(solution)/shard_map/all_to_all | solution.py:294
  33.1 0.0 all-gather.2.cloned.1.call-update
  33.2 0.1 collective-permute-start
  33.3 0.0 copy-start
  33.3 3.0 %shard_map.51 = (bf16[384,4096]{1,0:T(8,128)(2,1)S(1)}, f32[1,4096]{1,0:T(1,128)S(1)}) custom-call(f32[384,4096]{1,0:T(8,128)} %weight.3), custom_call_target="tpu_custom_call" | custom-call | flops 4718592 | bytes 6291456 | tf_op jit(solution)/shard_map/pallas_call | solution.py:300
  36.3 0.1 pad_add_fusion.where
  36.4 0.0 copy-start.2
  36.4 0.0 collective-permute-done.other
  36.4 0.0 copy-done
  36.4 2.9 %shard_map.52 = (f32[512,4096]{1,0:T(8,128)S(1)}, bf16[512,384]{1,0:T(8,128)(2,1)S(1)}, f32[8,32,128]{2,1,0:T(8,128)S(1)}) custom-call(s32[2]{0:T(128)S(1)} %pad_add_fusion.where, bf16[256,768]{1,0:T(8,128)(2,1)S(1)} %bitcast.9, bf16[256,768]{1,0:T(8,128)(2,1)S(1)} %collective-permute-done.other, bf16[384,4096]{1,0:T(8,128)(2,1)S(1)} %get-tuple-element.15.units), custom_call_target="tpu_custom_call" | custom-call | flops 1610612736 | tf_op jit(solution)/shard_map/pallas_call | solution.py:310
  39.3 12.4 %all_to_all.46.parts = f32[8,32,128]{2,1,0:T(8,128)S(1)} all-to-all(f32[8,32,128]{2,1,0:T(8,128)S(1)} %get-tuple-element.17), channel_id=1, replica_groups=mesh['crops'=8,'protos'=32] {'crops'}, dimensions={0} | all-to-all | bytes 262144 | tf_op jit(solution)/shard_map/all_to_all | solution.py:325
  51.8 1.2 shard_map.53
  53.0 0.0 copy-done.2
  53.0 15.5 %all_to_all.47.parts = f32[32,4,128]{2,1,0:T(4,128)S(1)} all-to-all(f32[32,4,128]{2,1,0:T(4,128)S(1)} %get-tuple-element.18), channel_id=1, replica_groups=mesh['crops'=8,'protos'=32] {'protos'}, dimensions={0} | all-to-all | bytes 131072 | tf_op jit(solution)/shard_map/all_to_all | solution.py:328
  68.5 0.8 shard_map.54
  69.3 11.1 %all_to_all.48.parts = f32[8,32,128]{2,1,0:T(8,128)S(1)} all-to-all(f32[8,32,128]{2,1,0:T(8,128)S(1)} %shard_map.54), channel_id=1, replica_groups=mesh['crops'=8,'protos'=32] {'crops'}, dimensions={0} | all-to-all | bytes 262144 | tf_op jit(solution)/shard_map/all_to_all | solution.py:325
  80.3 1.2 shard_map.55
  81.5 13.6 %all_to_all.49.parts = f32[32,4,128]{2,1,0:T(4,128)S(1)} all-to-all(f32[32,4,128]{2,1,0:T(4,128)S(1)} %get-tuple-element.19), channel_id=1, replica_groups=mesh['crops'=8,'protos'=32] {'protos'}, dimensions={0} | all-to-all | bytes 131072 | tf_op jit(solution)/shard_map/all_to_all | solution.py:328
  95.2 0.8 shard_map.56
  95.9 10.4 %all_to_all.50.parts = f32[8,32,128]{2,1,0:T(8,128)S(1)} all-to-all(f32[8,32,128]{2,1,0:T(8,128)S(1)} %shard_map.56), channel_id=1, replica_groups=mesh['crops'=8,'protos'=32] {'crops'}, dimensions={0} | all-to-all | bytes 262144 | tf_op jit(solution)/shard_map/all_to_all | solution.py:325
  106.4 0.0 copy-start.3
  106.4 3.9 %shard_map.57 = (f32[32,16,128]{2,1,0:T(8,128)S(1)}, f32[32,128]{1,0:T(8,128)S(1)}) custom-call(f32[512,4096]{1,0:T(8,128)S(1)} %get-tuple-element.16.table, f32[8,32,128]{2,1,0:T(8,128)S(1)} %all_to_all.50.parts, bf16[512,384]{1,0:T(8,128)(2,1)S(1)} %get-tuple-element.20.student, bf16[384,4096]{1,0:T(8,128)(2,1)S(1)} %get-tuple-element.15.units), custom_call_target="tpu_custom_call" | custom-call | flops 1610612736 | tf_op jit(solution)/shard_map/pallas_call | solution.py:350
  110.3 0.0 all-gather.2.cloned.1.call-done.mine
  110.3 0.3 collective-permute-start.1
  110.6 21.9 %all_to_all.51.parts = f32[32,16,128]{2,1,0:T(8,128)} all-to-all(f32[32,16,128]{2,1,0:T(8,128)S(1)} %get-tuple-element.25), channel_id=1, replica_groups=mesh['crops'=8,'protos'=32] {'protos'}, dimensions={0} | all-to-all | bytes 524288 | tf_op jit(solution)/shard_map/all_to_all | solution.py:328
  132.5 1.6 shard_map.58
  134.1 10.5 %all_to_all.52.factors = f32[8,8,128]{2,1,0:T(8,128)S(1)} all-to-all(f32[8,8,128]{2,1,0:T(8,128)} %get-tuple-element.26), channel_id=1, replica_groups=mesh['crops'=8,'protos'=32] {'crops'}, dimensions={0} | all-to-all | bytes 65536 | tf_op jit(solution)/shard_map/all_to_all | solution.py:325
  144.6 0.0 collective-permute-done.1.other
  144.6 0.0 copy-done.3
  144.6 12.2 %shard_map.59 = f32[8,48,512]{2,1,0:T(8,128)S(1)} custom-call(s32[2]{0:T(128)S(1)} %copy-done.3, bf16[2048,768]{1,0:T(8,128)(2,1)} %all-gather.2.cloned.1.call-done.mine, bf16[2048,768]{1,0:T(8,128)(2,1)} %collective-permute-done.1.other, bf16[384,4096]{1,0:T(8,128)(2,1)S(1)} %get-tuple-element.15.units, f32[384,4096]{1,0:T(8,128)} %weight.3, ...), custom_call_target="tpu_custom_call" | custom-call | flops 4831838208 | tf_op jit(solution)/shard_map/pallas_call | solution.py:371
  156.8 0.0 copy-start.1
  156.8 0.9 copy-done.1
  157.7 4.8 %all-to-all-start.8 = ((f32[8,48,512]{2,1,0:T(8,128)}), f32[8,48,512]{2,1,0:T(8,128)S(1)}, u32[]{:S(2)}, u32[]{:S(2)}) async-start(f32[8,48,512]{2,1,0:T(8,128)} %copy-done.1), calls=%async_computation.8 | async-start | bytes 1572864 | tf_op jit(solution)/shard_map/all_to_all | solution.py:391
  162.5 1.3 dynamic_slice.3
  163.7 8.8 %all-to-all-done.8 = f32[8,48,512]{2,1,0:T(8,128)S(1)} async-done(((f32[8,48,512]{2,1,0:T(8,128)}), f32[8,48,512]{2,1,0:T(8,128)S(1)}, u32[]{:S(2)}, u32[]{:S(2)}) %all-to-all-start.8) | async-done | bytes 786464 | tf_op jit(solution)/shard_map/all_to_all | solution.py:391
  172.6 0.9 copy.6
Async XLA Ops:
  7.2 103.1 %all-gather.2.cloned.1.call-start = ((), (), s32[]{:S(2)}) async-start(), calls=%async_computation.9 | async-start | bytes 3538944 | tf_op jit(solution)/shard_map/all_gather | solution.py:298
  33.2 3.3 %collective-permute-start = (bf16[256,768]{1,0:T(8,128)(2,1)}, bf16[256,768]{1,0:T(8,128)(2,1)S(1)}, u32[]{:S(2)}, u32[]{:S(2)}) collective-permute-start(bf16[256,768]{1,0:T(8,128)(2,1)} %bitcast.8), channel_id=1, source_target_pairs={{0,1},{1,0},{2,3},{3,2},{4,5},{5,4},{6,7},{7,6},{8,9},{9,8},{10,11... | collective-permute-start | bytes 1179656 | tf_op jit(solution)/shard_map/ppermute | solution.py:297
  33.3 3.1 %copy-start = (bf16[16,16,768]{2,1,0:T(8,128)(2,1)S(1)}, bf16[16,16,768]{2,1,0:T(8,128)(2,1)}, u32[]{:S(2)}) copy-start(bf16[16,16,768]{2,1,0:T(8,128)(2,1)} %all_to_all.45) | copy-start | bytes 1179652
  36.4 16.6 %copy-start.2 = (s32[2]{0:T(128)}, s32[2]{0:T(128)S(1)}, u32[]{:S(2)}) copy-start(s32[2]{0:T(128)S(1)} %pad_add_fusion.where) | copy-start | bytes 28
  106.4 38.2 %copy-start.3 = (s32[2]{0:T(128)S(1)}, s32[2]{0:T(128)}, u32[]{:S(2)}) copy-start(s32[2]{0:T(128)} %copy-done.2) | copy-start | bytes 28
  110.3 34.3 %collective-permute-start.1 = (bf16[2048,768]{1,0:T(8,128)(2,1)}, bf16[2048,768]{1,0:T(8,128)(2,1)}, u32[]{:S(2)}, u32[]{:S(2)}) collective-permute-start(bf16[2048,768]{1,0:T(8,128)(2,1)} %all-gather.2.cloned.1.call-done.mine), channel_id=1, source_target_pairs={{0,1},{1,0},{2,3},{3,2},{4,5},{5,4},{6,7},{7,6},{8,9},{9,8},{10,11... | collective-permute-start | bytes 9437192 | tf_op jit(solution)/shard_map/ppermute | solution.py:361
  156.8 0.9 copy-start.1
  157.7 14.9 %all-to-all-start.8 = ((f32[8,48,512]{2,1,0:T(8,128)}), f32[8,48,512]{2,1,0:T(8,128)S(1)}, u32[]{:S(2)}, u32[]{:S(2)}) async-start(f32[8,48,512]{2,1,0:T(8,128)} %copy-done.1), calls=%async_computation.8 | async-start | bytes 1572864 | tf_op jit(solution)/shard_map/all_to_all | solution.py:391
Sparse Core Ops, SparseCore 0:
  33.3 75.8 all-gather.1

commit v2 on v1

v2 whole, which is shorter than its diff:
```python
import functools
import math

import jax
import jax.numpy as jnp
from jax import lax
from jax.experimental import pallas as pl
from jax.experimental.pallas import tpu as pltpu
from jax.sharding import PartitionSpec as P

D = 384
PROTOS = 131072
CROPS = 4096
LOSS_SCALE = 8192
LANES = 128
MIB = 1 << 20
F32 = jnp.float32
BF16 = jnp.bfloat16
HIGHEST = lax.Precision.HIGHEST
TEACHER = math.log2(math.e) / 0.07
STUDENT = 1.0 / 0.1
LOG2E = math.log2(math.e)
VMEM = pl.BlockSpec(memory_space=pltpu.VMEM)
SMEM = pl.BlockSpec(memory_space=pltpu.SMEM)
HBM = pl.BlockSpec(memory_space=pltpu.HBM)


def params(mib=14):
    return pltpu.CompilerParams(vmem_limit_bytes=mib * MIB)


def pinned(x):
    return pltpu.with_memory_space_constraint(x, pltpu.VMEM)


def in_hbm(x):
    return pltpu.with_memory_space_constraint(x, pltpu.HBM)


def cost(flops=0, read=0, exps=0):
    return pl.CostEstimate(flops=int(flops), bytes_accessed=int(read), transcendentals=int(exps))


def unit(values):
    wide = values.astype(F32)
    return (wide * lax.rsqrt(jnp.sum(wide * wide, axis=1, keepdims=True) + 1e-6)).astype(BF16)


def own_kernel(teacher, student, out, held, sems):
    copies = [
        pltpu.make_async_copy(x, held.at[n], sems.at[n]) for n, x in enumerate((teacher, student))
    ]
    for copy in copies:
        copy.start()
    for copy in copies:
        copy.wait()
    rows = jnp.concatenate([unit(held[0]), unit(held[1])], axis=1)
    for k in range(out.shape[0]):
        out[k] = rows


def prep_kernel(where, weight, units, inverse, share, held, sems):
    blocks = held.shape[0]
    width = held.shape[2]
    copies = []
    for k in range(blocks):
        copy = pltpu.make_async_copy(weight.at[:, pl.ds(k * width, width)], held.at[k], sems.at[k])
        copy.start()
        copies.append(copy)
    for k in range(blocks):
        copies[k].wait()
        total = jnp.zeros((8, width), F32)
        for d in range(0, D, 8):
            part = held[k, d : d + 8, :]
            total += part * part
        inv = lax.rsqrt(jnp.sum(total, axis=0, keepdims=True) + 1e-6)
        inverse[:, k * width : (k + 1) * width] = inv
        for d in range(0, D, 16):
            units[d : d + 16, k * width : (k + 1) * width] = (held[k, d : d + 16, :] * inv).astype(BF16)
    count = share.shape[0]
    begin = pl.multiple_of(where[1] * count, count)
    share[...] = jnp.transpose(units[:, pl.ds(begin, count)])


def col_rows(total, sums, start):
    for t in range(sums.shape[1] // LANES):
        total[start + t : start + t + 1, :] = sums[:, t * LANES : (t + 1) * LANES]


def exp_rows(rows, start, units, table, student, total):
    half = rows.shape[0]
    student[pl.ds(start, half), :] = rows[:, D:]
    width = 512
    for k in range(table.shape[1] // width):
        cols = slice(k * width, (k + 1) * width)
        e = jnp.exp2(jnp.dot(rows[:, :D], units[:, cols], preferred_element_type=F32) * TEACHER)
        table[pl.ds(start, half), cols] = e
        sums = e[0:8, :]
        for d in range(8, half, 8):
            sums += e[d : d + 8, :]
        col_rows(total, jnp.sum(sums, axis=0, keepdims=True), k * width // LANES)


def exp_mine_kernel(where, mine, units, table, student, total, held, sem):
    copy = pltpu.make_async_copy(mine, held, sem)
    copy.start()
    copy.wait()
    half = held.shape[0]
    exp_rows(held, pl.multiple_of(where[0] * half, half), units, table, student, total)


def exp_other_kernel(where, other, units, first, _, __, table, student, out, total):
    half = other.shape[0]
    exp_rows(other, pl.multiple_of((1 - where[0]) * half, half), units, table, student, total)
    every = first[...] + total[...]
    for k in range(out.shape[0]):
        out[k] = every


def col_scales(parts, scale):
    scale[...] = 1.0 / (PROTOS * jnp.sum(parts[...], axis=0))


def lane_sums(acc):
    ones = jnp.ones((8, LANES), F32)
    sums = lax.dot_general(
        ones, acc, (((1,), (1,)), ((), ())), precision=HIGHEST, preferred_element_type=F32
    )
    return sums[0:1, :]


def row_kernel(table, parts, out, scale, acc, total):
    col_scales(parts, scale)
    rows, cols = table.shape
    step = 64
    for i in range(0, rows, step):
        sums = jnp.zeros((step, LANES), F32)
        for j in range(cols // LANES):
            sums += table[i : i + step, j * LANES : (j + 1) * LANES] * scale[j : j + 1, :]
        acc[i : i + step, :] = sums
    col_rows(total, lane_sums(acc[...]), 0)
    every = total[...]
    for k in range(out.shape[0]):
        out[k] = every


def down(vector):
    return jnp.transpose(jnp.broadcast_to(vector, (LANES, LANES)))


def col_kernel(table, parts, out, weight, total):
    rows, cols = table.shape
    scale = 1.0 / (CROPS * jnp.sum(parts[...], axis=0))
    for t in range(rows // LANES):
        weight[t * LANES : (t + 1) * LANES, :] = down(scale[t : t + 1, :])
    tiles = 8
    for j in range(0, cols, tiles * LANES):
        sums = [jnp.zeros((8, LANES), F32) for _ in range(tiles)]
        for i in range(0, rows, 8):
            w = weight[i : i + 8, :]
            for t in range(tiles):
                sums[t] += table[i : i + 8, j + t * LANES : j + (t + 1) * LANES] * w
        for t in range(tiles):
            row = j // LANES + t
            total[row : row + 1, :] = jnp.sum(sums[t], axis=0, keepdims=True)
    every = total[...]
    for k in range(out.shape[0]):
        out[k] = every


def last_kernel(table, parts, student, units, out, scale, acc):
    col_scales(parts, scale)
    rows, cols = table.shape
    acc[...] = jnp.zeros_like(acc)
    width = 512
    step = 256
    for k in range(0, cols, width):
        for i in range(0, rows, step):
            z = jnp.dot(
                student[i : i + step, :], units[:, k : k + width], preferred_element_type=F32
            )
            x = jnp.exp2(z * (STUDENT * LOG2E))
            plain = cross = exps = None
            for t in range(width // LANES):
                j = k // LANES + t
                here = slice(t * LANES, (t + 1) * LANES)
                e = table[i : i + step, j * LANES : (j + 1) * LANES] * scale[j : j + 1, :]
                zt, xt = z[:, here], x[:, here]
                plain = e if t == 0 else plain + e
                cross = e * zt if t == 0 else cross + e * zt
                exps = xt if t == 0 else exps + xt
            acc[0, i : i + step, :] += plain
            acc[1, i : i + step, :] += cross
            acc[2, i : i + step, :] += exps
    every = jnp.concatenate([lane_sums(acc[0]), lane_sums(acc[2])], axis=1)
    cross = lane_sums(acc[1]) * STUDENT
    count = out.shape[0]
    own = rows // count
    for k in range(count):
        tile = first_crop(k, rows // 2, own) // LANES
        out[k, :, : 2 * rows] = every
        out[k, :, 2 * rows :] = cross[:, tile * LANES : (tile + 1) * LANES]


def first_crop(number, half, own):
    return (number & 1) * half + (number >> 1) * own


def loss_kernel(where, parts, out, loss, held):
    sums = parts[0]
    for k in range(1, parts.shape[0]):
        sums += parts[k]
    rows = out.shape[2] // 2
    held[...] = sums
    first = where[2]
    tile = pl.multiple_of(first // LANES * LANES, LANES)
    plain = held[:, pl.ds(tile, LANES)]
    exps = held[:, pl.ds(rows + tile, LANES)]
    row = jnp.log(exps) - sums[:, 2 * rows :] / plain
    loss[...] = pltpu.roll(row, (LANES - first % LANES) % LANES, 1)[:, : loss.shape[1]]
    every = (LOSS_SCALE / 0.1) / sums[:, : 2 * rows]
    for k in range(out.shape[0]):
        out[k] = every


def grad_kernel(
    order, where, mine, other, units, weight, inverse, scale, factors, out,
    held, logits, wsub, csub, turned, grad, sems, wsem,
):
    core, place = where[0], where[1]
    groups = factors.shape[0]
    rows = factors.shape[2] // 2
    width = wsub.shape[1]
    half = mine.shape[0] // groups
    begin = pl.multiple_of(place * width, width)
    copies = []
    for n in range(groups):
        here = pl.ds(n * half, half)
        copies.append(pltpu.make_async_copy(mine.at[here, :], held.at[here, :], sems.at[n]))
        copies[-1].start()
    wcopy = pltpu.make_async_copy(weight.at[:, pl.ds(begin, width)], wsub, wsem)
    wcopy.start()
    inv = inverse[:, pl.ds(begin, width)]
    tiles = width // LANES
    for t in range(tiles):
        csub[t * LANES : (t + 1) * LANES, :] = down(scale[pl.ds(place * tiles + t, 1), :])
    nt = (((1,), (1,)), ((), ()))
    last = 2 * groups

    def crops_of(c, here):
        n = c % groups
        return (other if c < groups else held)[n * half : (n + 1) * half, here]

    def products(c):
        for k in range(2):
            logits[c % 2, k] = lax.dot_general(
                units[...], crops_of(c, slice(k * D, (k + 1) * D)), nt, preferred_element_type=F32
            )

    products(0)
    for c in range(last):
        if c + 1 == groups:
            for copy in copies:
                copy.wait()
        if c + 1 < last:
            products(c + 1)
        owner = 1 - core if c < groups else core
        group = order[c % groups]
        parts = []
        for t in range(0, half, LANES):
            at = pl.multiple_of(owner * half, half) + t
            a = factors[group, :, pl.ds(at, LANES)]
            b = factors[group, :, pl.ds(rows + at, LANES)]
            here = slice(t, t + LANES)
            x = jnp.exp2(logits[c % 2, 1, :, here] * (STUDENT * LOG2E)) * b
            e = jnp.exp2(logits[c % 2, 0, :, here] * TEACHER) * (csub[...] * a)
            parts.append((x - e).astype(BF16))
        part = jnp.dot(
            jnp.concatenate(parts, axis=1),
            crops_of(c, slice(D, 2 * D)),
            preferred_element_type=F32,
        )
        turned[...] = part if c == 0 else turned[...] + part
    for t in range(tiles):
        for d in range(0, D, LANES):
            grad[d : d + LANES, t * LANES : (t + 1) * LANES] = jnp.transpose(
                turned[t * LANES : (t + 1) * LANES, d : d + LANES]
            )
    wcopy.wait()
    inner = jnp.zeros((8, width), F32)
    for d in range(0, D, 8):
        inner += wsub[d : d + 8, :] * inv * grad[d : d + 8, :]
    inner = jnp.sum(inner, axis=0, keepdims=True)
    share = out.shape[1]
    for d in range(0, D, 8):
        cu = wsub[d : d + 8, :] * inv
        out[d // share, d % share : d % share + 8, :] = (grad[d : d + 8, :] - cu * inner) * inv


def struct(shape, dtype=F32):
    return jax.ShapeDtypeStruct(shape, dtype)


def local(teacher_feats, student_feats, proto_weight):
    crops, protos = lax.axis_size("crops"), lax.axis_size("protos")
    own = teacher_feats.shape[0]
    rows = own * protos
    half = rows // 2
    cols = proto_weight.shape[1]
    width = cols // crops
    share = D // crops
    ctile, rtile = cols // LANES, rows // LANES
    number = lax.axis_index("protos")
    place = lax.axis_index("crops")
    first = first_crop(number, half, own)
    where = jnp.stack([number & 1, place, first]).astype(jnp.int32)
    swap = [(j, j ^ 1) for j in range(protos)]
    same_core = [[j for j in range(protos) if j % 2 == core] for core in range(2)]
    ring = list(range(0, crops, 2)) + list(range(crops - 1, 0, -2))

    def over_crops(x):
        return lax.all_to_all(x, "crops", 0, 0, tiled=True)

    def over_protos(x):
        return lax.all_to_all(x, "protos", 0, 0, tiled=True)

    copies = pl.pallas_call(
        own_kernel,
        out_shape=pltpu.VMEM((protos // 2, own, 2 * D), BF16),
        in_specs=[HBM, HBM],
        out_specs=VMEM,
        scratch_shapes=[pltpu.VMEM((2, own, D), BF16), pltpu.SemaphoreType.DMA((2,))],
        compiler_params=params(),
        cost_estimate=cost(rows * D, 2 * rows * D),
    )(in_hbm(teacher_feats), in_hbm(student_feats))
    mine = lax.all_to_all(
        copies, "protos", 0, 0, tiled=True, axis_index_groups=same_core
    ).reshape(half, 2 * D)

    units, inverse, share_units = pl.pallas_call(
        prep_kernel,
        out_shape=(
            pltpu.VMEM((D, cols), BF16),
            pltpu.VMEM((1, cols), F32),
            pltpu.VMEM((width, D), BF16),
        ),
        in_specs=[SMEM, HBM],
        out_specs=(VMEM, VMEM, VMEM),
        scratch_shapes=[pltpu.VMEM((8, D, cols // 8), F32), pltpu.SemaphoreType.DMA((8,))],
        compiler_params=params(),
        cost_estimate=cost(3 * D * cols, 4 * D * cols),
    )(where, in_hbm(proto_weight))
    mine, inverse = lax.optimization_barrier((mine, inverse))
    other = lax.ppermute(mine, "protos", swap)
    all_mine = lax.all_gather(mine, "crops", axis=0, tiled=True, axis_index_groups=[ring])

    table, student, total = pl.pallas_call(
        exp_mine_kernel,
        out_shape=(
            pltpu.VMEM((rows, cols), F32),
            pltpu.VMEM((rows, D), BF16),
            pltpu.VMEM((ctile, LANES), F32),
        ),
        in_specs=[SMEM, HBM, VMEM],
        out_specs=(VMEM, VMEM, VMEM),
        scratch_shapes=[pltpu.VMEM((half, 2 * D), BF16), pltpu.SemaphoreType.DMA],
        compiler_params=params(),
        cost_estimate=cost(rows * D * cols, 0, rows * cols // 2),
    )(where, in_hbm(mine), pinned(units))
    table, student, parts = pl.pallas_call(
        exp_other_kernel,
        out_shape=(
            pltpu.VMEM((rows, cols), F32),
            pltpu.VMEM((rows, D), BF16),
            struct((crops, ctile, LANES)),
        ),
        in_specs=[SMEM] + [VMEM] * 5,
        out_specs=(VMEM, VMEM, VMEM),
        input_output_aliases={4: 0, 5: 1},
        scratch_shapes=[pltpu.VMEM((ctile, LANES), F32)],
        compiler_params=params(),
        cost_estimate=cost(rows * D * cols, 0, rows * cols // 2),
    )(where, other, pinned(units), pinned(total), pinned(table), pinned(student))

    for step in range(2):
        rparts, _ = pl.pallas_call(
            row_kernel,
            out_shape=(struct((protos, rtile, LANES)), struct((ctile, LANES))),
            in_specs=[VMEM, VMEM],
            out_specs=(VMEM, VMEM),
            scratch_shapes=[pltpu.VMEM((rows, LANES), F32), pltpu.VMEM((rtile, LANES), F32)],
            compiler_params=params(),
            cost_estimate=cost(2 * rows * cols),
        )(pinned(table), over_crops(parts))
        parts = pl.pallas_call(
            col_kernel,
            out_shape=struct((crops, ctile, LANES)),
            in_specs=[VMEM, VMEM],
            out_specs=VMEM,
            scratch_shapes=[pltpu.VMEM((rows, LANES), F32), pltpu.VMEM((ctile, LANES), F32)],
            compiler_params=params(),
            cost_estimate=cost(2 * rows * cols),
        )(pinned(table), over_protos(rparts))

    rparts, scale = pl.pallas_call(
        last_kernel,
        out_shape=(struct((protos, 1, 2 * rows + LANES)), struct((ctile, LANES))),
        in_specs=[VMEM, VMEM, VMEM, VMEM],
        out_specs=(VMEM, VMEM),
        scratch_shapes=[pltpu.VMEM((3, rows, LANES), F32)],
        compiler_params=params(),
        cost_estimate=cost(2 * rows * D * cols, 0, rows * cols),
    )(pinned(table), over_crops(parts), pinned(student), pinned(units))
    all_mine, rparts = lax.optimization_barrier((all_mine, rparts))
    all_other = lax.ppermute(all_mine, "protos", swap)
    factors, loss = pl.pallas_call(
        loss_kernel,
        out_shape=(pltpu.VMEM((crops, 1, 2 * rows), F32), struct((1, own))),
        in_specs=[SMEM, VMEM],
        out_specs=(VMEM, VMEM),
        scratch_shapes=[pltpu.VMEM((1, 2 * rows + LANES), F32)],
        compiler_params=params(),
    )(where, over_protos(rparts))

    grad = pl.pallas_call(
        functools.partial(grad_kernel, ring),
        out_shape=pltpu.VMEM((crops, share, width), F32),
        in_specs=[SMEM, HBM, VMEM, VMEM, HBM, VMEM, VMEM, VMEM],
        out_specs=VMEM,
        scratch_shapes=[
            pltpu.VMEM((crops * half, 2 * D), BF16),
            pltpu.VMEM((2, 2, width, half), F32),
            pltpu.VMEM((D, width), F32),
            pltpu.VMEM((width, LANES), F32),
            pltpu.VMEM((width, D), F32),
            pltpu.VMEM((D, width), F32),
            pltpu.SemaphoreType.DMA((crops,)),
            pltpu.SemaphoreType.DMA,
        ],
        compiler_params=params(20),
        cost_estimate=cost(6 * CROPS * D * width, 0, 2 * CROPS * width),
    )(
        where, in_hbm(all_mine), pinned(all_other), pinned(share_units), in_hbm(proto_weight),
        pinned(inverse), scale, over_crops(factors),
    )
    moved = over_crops(grad)
    weight_grad = moved.transpose(1, 0, 2).reshape(share, cols)
    return (weight_grad, loss.reshape(own))


def solution(mesh):
    placed = (P(("crops", "protos"), None), P(("crops", "protos"), None), P(None, "protos"))
    return jax.shard_map(
        local,
        mesh=mesh,
        in_specs=placed,
        out_specs=(P("crops", "protos"), P(("crops", "protos"))),
        check_vma=False,
    )
```

time: 181 us -> 163 us (0.901)
  blocking collectives: 120 us -> 98.5 us
  starting transfers between devices: 5.22 us -> 10.6 us
  Pallas kernels: 29.2 us -> 27.2 us
    all_to_all x1 -> x0, blocking collectives: 24.4 us -> none  [local(): lax.all_to_all(copies, 'protos', 0, 0, tiled=True, axis_index_groups=same...]
    all_to_all x4 -> x5, blocking collectives: 44.4 us -> 54.3 us  [over_crops(): return lax.all_to_all(x, 'crops', 0, 0, tiled=True)]
    all_to_all x3, blocking collectives: 51.1 us -> 44.2 us  [over_protos(): return lax.all_to_all(x, 'protos', 0, 0, tiled=True)]
    all_to_all x1, starting transfers between devices: 4.82 us -> 10.2 us  [local(): lax.all_to_all(copies, 'protos', 0, 0, tiled=True, axis_index_groups=same...]
    pallas_call x5 -> x6, Pallas kernels: 22.2 us -> 19.2 us  [the longest x1 8.03 us: local(): pl.pallas_call(functools.partial(grad_kernel, ring), out_shape=pltpu.VMEM...]
  transfers between devices with their start and end apart: 4 -> 4, of which waited for: 1 -> 1; matrix products, arithmetic and copies ran while one was open for 1% -> 0% of each run, Pallas kernels for 9% -> 11%
where the time goes in v2:
time: 163 us
  blocking collectives  98.5 us (60%)
  Pallas kernels  27.2 us (17%)
  between operations  14.1 us (9%)
  starting transfers between devices  10.6 us (7%)
  waiting for transfers between devices  9.63 us (6%)
  local copies, waits for them, and re-layouts  2.7 us (2%)
    all_to_all x5, blocking collectives, over_crops(): return lax.all_to_all(x, 'crops', 0, 0, tiled=True)  54.3 us
    all_to_all x3, blocking collectives, over_protos(): return lax.all_to_all(x, 'protos', 0, 0, tiled=True)  44.2 us
    all_to_all x1, starting transfers between devices, local(): lax.all_to_all(copies, 'protos', 0, 0, tiled=True, axis_index_groups=same...  10.2 us
    all_to_all x1, waiting for transfers between devices, local(): lax.all_to_all(copies, 'protos', 0, 0, tiled=True, axis_index_groups=same...  9.58 us
    pallas_call x1, Pallas kernels, local(): pl.pallas_call(functools.partial(grad_kernel, ring), out_shape=pltpu.VMEM...  8.03 us
    pallas_call x1, Pallas kernels, local(): pl.pallas_call(last_kernel, out_shape=(struct((protos, 1, 2 * rows + LANE...  3.77 us
    pallas_call x1, Pallas kernels, local(): pl.pallas_call(prep_kernel, out_shape=(pltpu.VMEM((D, cols), BF16), pltpu...  3.69 us
  transfers between devices with their start and end apart: 4, of which 1 were waited for; matrix products, arithmetic and copies ran while one was open for 0% of the time, Pallas kernels for 11%

profile of v2, /device:TPU:2, one launch (start us, length us, event | category | flops | bytes accessed | tf_op | source)
XLA Modules:
  0.0 162.8 jit_solution(15974666075428367344)
XLA Ops:
  7.2 1.6 shard_map.50
  8.8 10.2 %all-to-all-start = ((bf16[16,16,768]{2,1,0:T(8,128)(2,1)}), bf16[16,16,768]{2,1,0:T(8,128)(2,1)}, u32[]{:S(2)}, u32[]{:S(2)}) async-start(bf16[16,16,768]{2,1,0:T(8,128)(2,1)} %shard_map.50), calls=%async_computation | async-start | bytes 786432 | tf_op jit(solution)/shard_map/all_to_all | solution.py:336
  19.0 0.0 all-gather.2.cloned.1.call-start
  19.0 0.1 pad_add_fusion.where
  19.1 3.7 %shard_map.51 = (bf16[384,4096]{1,0:T(8,128)(2,1)S(1)}, f32[1,4096]{1,0:T(1,128)S(1)}, bf16[512,384]{1,0:T(8,128)(2,1)S(1)}) custom-call(s32[3]{0:T(128)S(1)} %pad_add_fusion.where, f32[384,4096]{1,0:T(8,128)} %weight.3), custom_call_target="tpu_custom_call" | custom-call | flops 4718592 | bytes 6291456 | tf_op jit(solution)/shard_map/pallas_call | solution.py:340
  22.8 0.0 copy-start
  22.8 0.8 copy-done
  23.6 9.6 %all-to-all-done = bf16[16,16,768]{2,1,0:T(8,128)(2,1)} async-done(((bf16[16,16,768]{2,1,0:T(8,128)(2,1)}), bf16[16,16,768]{2,1,0:T(8,128)(2,1)}, u32[]{:S(2)}, u32[]{:S(2)}) %all-to-all-start) | async-done | bytes 393248 | tf_op jit(solution)/shard_map/all_to_all | solution.py:336
  33.1 0.0 all-gather.2.cloned.1.call-update
  33.2 0.1 collective-permute-start
  33.3 2.8 %shard_map.52 = (f32[512,4096]{1,0:T(8,128)S(1)}, bf16[512,384]{1,0:T(8,128)(2,1)S(1)}, f32[32,128]{1,0:T(8,128)S(1)}) custom-call(s32[3]{0:T(128)S(1)} %pad_add_fusion.where, bf16[256,768]{1,0:T(8,128)(2,1)} %bitcast.3.mine, bf16[384,4096]{1,0:T(8,128)(2,1)S(1)} %get-tuple-element.23.units), custom_call_target="tpu_custom_call" | custom-call | flops 805306368 | tf_op jit(solution)/shard_map/pallas_call | solution.py:357
  36.1 0.0 collective-permute-done.other
  36.1 1.8 %shard_map.53 = (f32[512,4096]{1,0:T(8,128)S(1)}, bf16[512,384]{1,0:T(8,128)(2,1)S(1)}, f32[8,32,128]{2,1,0:T(8,128)S(1)}) custom-call(s32[3]{0:T(128)S(1)} %pad_add_fusion.where, bf16[256,768]{1,0:T(8,128)(2,1)S(1)} %collective-permute-done.other, bf16[384,4096]{1,0:T(8,128)(2,1)S(1)} %get-tuple-element.23.units, ...), custom_call_target="tpu_custom_call", output_to_operand_aliasing={{0}: (4, {}), {1}: (5, {})} | custom-call | flops 805306368 | tf_op jit(solution)/shard_map/pallas_call | solution.py:370
  37.9 12.0 %all_to_all.45.parts = f32[8,32,128]{2,1,0:T(8,128)S(1)} all-to-all(f32[8,32,128]{2,1,0:T(8,128)S(1)} %get-tuple-element.28), channel_id=1, replica_groups=mesh['crops'=8,'protos'=32] {'crops'}, dimensions={0} | all-to-all | bytes 262144 | tf_op jit(solution)/shard_map/all_to_all | solution.py:322
  49.9 1.3 shard_map.54
  51.3 15.4 %all_to_all.46.parts = f32[32,4,128]{2,1,0:T(4,128)S(1)} all-to-all(f32[32,4,128]{2,1,0:T(4,128)S(1)} %get-tuple-element.29), channel_id=1, replica_groups=mesh['crops'=8,'protos'=32] {'protos'}, dimensions={0} | all-to-all | bytes 131072 | tf_op jit(solution)/shard_map/all_to_all | solution.py:325
  66.7 0.8 shard_map.55
  67.4 10.5 %all_to_all.47.parts = f32[8,32,128]{2,1,0:T(8,128)S(1)} all-to-all(f32[8,32,128]{2,1,0:T(8,128)S(1)} %shard_map.55), channel_id=1, replica_groups=mesh['crops'=8,'protos'=32] {'crops'}, dimensions={0} | all-to-all | bytes 262144 | tf_op jit(solution)/shard_map/all_to_all | solution.py:322
  78.0 1.3 shard_map.56
  79.3 13.5 %all_to_all.48.parts = f32[32,4,128]{2,1,0:T(4,128)S(1)} all-to-all(f32[32,4,128]{2,1,0:T(4,128)S(1)} %get-tuple-element.30), channel_id=1, replica_groups=mesh['crops'=8,'protos'=32] {'protos'}, dimensions={0} | all-to-all | bytes 131072 | tf_op jit(solution)/shard_map/all_to_all | solution.py:325
  92.9 0.8 shard_map.57
  93.7 9.6 %all_to_all.49.parts = f32[8,32,128]{2,1,0:T(8,128)S(1)} all-to-all(f32[8,32,128]{2,1,0:T(8,128)S(1)} %shard_map.57), channel_id=1, replica_groups=mesh['crops'=8,'protos'=32] {'crops'}, dimensions={0} | all-to-all | bytes 262144 | tf_op jit(solution)/shard_map/all_to_all | solution.py:322
  103.3 3.8 %shard_map.58 = (f32[32,1,1152]{2,1,0:T(1,128)S(1)}, f32[32,128]{1,0:T(8,128)S(1)}) custom-call(f32[512,4096]{1,0:T(8,128)S(1)} %get-tuple-element.27.table, f32[8,32,128]{2,1,0:T(8,128)S(1)} %all_to_all.49.parts, bf16[512,384]{1,0:T(8,128)(2,1)S(1)} %get-tuple-element.31.student, bf16[384,4096]{1,0:T(8,128)(2,1)S(1)} %get-tuple-element.23.units), custom_call_target="tpu_custom_call" | custom-call | flops 1610612736 | tf_op jit(solution)/shard_map/pallas_call | solution.py:405
  107.1 0.0 all-gather.2.cloned.1.call-done.mine
  107.1 0.3 collective-permute-start.1
  107.4 15.3 %all_to_all.50.parts = f32[32,1,1152]{2,1,0:T(1,128)S(1)} all-to-all(f32[32,1,1152]{2,1,0:T(1,128)S(1)} %get-tuple-element.37), channel_id=1, replica_groups=mesh['crops'=8,'protos'=32] {'protos'}, dimensions={0} | all-to-all | bytes 294912 | tf_op jit(solution)/shard_map/all_to_all | solution.py:325
  122.6 1.2 shard_map.59
  123.8 8.6 %all_to_all.51.factors = f32[8,1,1024]{2,1,0:T(1,128)S(1)} all-to-all(f32[8,1,1024]{2,1,0:T(1,128)S(1)} %get-tuple-element.38), channel_id=1, replica_groups=mesh['crops'=8,'protos'=32] {'crops'}, dimensions={0} | all-to-all | bytes 65536 | tf_op jit(solution)/shard_map/all_to_all | solution.py:322
  132.4 0.0 collective-permute-done.1.other
  132.4 0.0 copy-start.1
  132.4 1.0 copy-done.1
  133.4 8.0 %shard_map.60 = f32[8,48,512]{2,1,0:T(8,128)S(1)} custom-call(s32[3]{0:T(128)S(1)} %pad_add_fusion.where, bf16[2048,768]{1,0:T(8,128)(2,1)} %all-gather.2.cloned.1.call-done.mine, bf16[2048,768]{1,0:T(8,128)(2,1)S(1)} %collective-permute-done.1.other, bf16[512,384]{1,0:T(8,128)(2,1)S(1)} %copy-done.1, f32[384,4096]{1,0:T(8,128)} %weight.3, ...), custom_call_target="tpu_custom_call" | custom-call | flops 4831838208 | tf_op jit(solution)/shard_map/pallas_call | solution.py:425
  141.4 13.6 %all_to_all.52 = f32[8,48,512]{2,1,0:T(8,128)S(1)} all-to-all(f32[8,48,512]{2,1,0:T(8,128)S(1)} %shard_map.60), channel_id=1, replica_groups=mesh['crops'=8,'protos'=32] {'crops'}, dimensions={0} | all-to-all | bytes 1572864 | tf_op jit(solution)/shard_map/all_to_all | solution.py:322
  155.0 0.9 copy.8
Async XLA Ops:
  8.8 24.4 %all-to-all-start = ((bf16[16,16,768]{2,1,0:T(8,128)(2,1)}), bf16[16,16,768]{2,1,0:T(8,128)(2,1)}, u32[]{:S(2)}, u32[]{:S(2)}) async-start(bf16[16,16,768]{2,1,0:T(8,128)(2,1)} %shard_map.50), calls=%async_computation | async-start | bytes 786432 | tf_op jit(solution)/shard_map/all_to_all | solution.py:336
  19.0 88.1 %all-gather.2.cloned.1.call-start = ((), (), s32[]{:S(2)}) async-start(), calls=%async_computation.9 | async-start | bytes 3538944 | tf_op jit(solution)/shard_map/all_gather | solution.py:355
  22.8 0.8 copy-start
  33.2 2.9 %collective-permute-start = (bf16[256,768]{1,0:T(8,128)(2,1)}, bf16[256,768]{1,0:T(8,128)(2,1)S(1)}, u32[]{:S(2)}, u32[]{:S(2)}) collective-permute-start(bf16[256,768]{1,0:T(8,128)(2,1)} %bitcast.3.mine), channel_id=1, source_target_pairs={{0,1},{1,0},{2,3},{3,2},{4,5},{5,4},{6,7},{7,6},{8,9},{9,8},{10,11... | collective-permute-start | bytes 1179656 | tf_op jit(solution)/shard_map/ppermute | solution.py:354
  107.1 25.3 %collective-permute-start.1 = (bf16[2048,768]{1,0:T(8,128)(2,1)}, bf16[2048,768]{1,0:T(8,128)(2,1)S(1)}, u32[]{:S(2)}, u32[]{:S(2)}) collective-permute-start(bf16[2048,768]{1,0:T(8,128)(2,1)} %all-gather.2.cloned.1.call-done.mine), channel_id=1, source_target_pairs={{0,1},{1,0},{2,3},{3,2},{4,5},{5,4},{6,7},{7,6},{8,9},{9,8},{10,11... | collective-permute-start | bytes 9437192 | tf_op jit(solution)/shard_map/ppermute | solution.py:415
  132.4 1.0 copy-start.1
Sparse Core Ops, SparseCore 0:
  33.3 43.3 all-gather.1

commit v3 on v2

--- a/solution.py
+++ b/solution.py
@@ -16,6 +16,7 @@
 MIB = 1 << 20
 F32 = jnp.float32
 BF16 = jnp.bfloat16
+SPARE = 16
 HIGHEST = lax.Precision.HIGHEST
 TEACHER = math.log2(math.e) / 0.07
 STUDENT = 1.0 / 0.1
@@ -59,7 +60,7 @@
         out[k] = rows
 
 
-def prep_kernel(where, weight, units, inverse, share, held, sems):
+def prep_kernel(weight, units, inverse, held, sems):
     blocks = held.shape[0]
     width = held.shape[2]
     copies = []
@@ -77,10 +78,6 @@
         inverse[:, k * width : (k + 1) * width] = inv
         for d in range(0, D, 16):
             units[d : d + 16, k * width : (k + 1) * width] = (held[k, d : d + 16, :] * inv).astype(BF16)
-    count = share.shape[0]
-    begin = pl.multiple_of(where[1] * count, count)
-    share[...] = jnp.transpose(units[:, pl.ds(begin, count)])
-
 
 def col_rows(total, sums, start):
     for t in range(sums.shape[1] // LANES):
@@ -93,7 +90,7 @@
     width = 512
     for k in range(table.shape[1] // width):
         cols = slice(k * width, (k + 1) * width)
-        e = jnp.exp2(jnp.dot(rows[:, :D], units[:, cols], preferred_element_type=F32) * TEACHER)
+        e = jnp.exp2(jnp.dot(rows[:, :D], units[:D, cols], preferred_element_type=F32) * TEACHER)
         table[pl.ds(start, half), cols] = e
         sums = e[0:8, :]
         for d in range(8, half, 8):
@@ -177,7 +174,7 @@
     for k in range(0, cols, width):
         for i in range(0, rows, step):
             z = jnp.dot(
-                student[i : i + step, :], units[:, k : k + width], preferred_element_type=F32
+                student[i : i + step, :], units[:D, k : k + width], preferred_element_type=F32
             )
             x = jnp.exp2(z * (STUDENT * LOG2E))
             plain = cross = exps = None
@@ -206,28 +203,30 @@
     return (number & 1) * half + (number >> 1) * own
 
 
-def loss_kernel(where, parts, out, loss, held):
-    sums = parts[0]
+def factor_kernel(where, parts, out, loss, sums):
+    total = parts[0]
     for k in range(1, parts.shape[0]):
-        sums += parts[k]
+        total += parts[k]
+    sums[...] = total
     rows = out.shape[2] // 2
-    held[...] = sums
+    every = (LOSS_SCALE / 0.1) / total[:, : 2 * rows]
+    for k in range(out.shape[0]):
+        out[k] = every
     first = where[2]
     tile = pl.multiple_of(first // LANES * LANES, LANES)
-    plain = held[:, pl.ds(tile, LANES)]
-    exps = held[:, pl.ds(rows + tile, LANES)]
-    row = jnp.log(exps) - sums[:, 2 * rows :] / plain
+    plain = sums[:, pl.ds(tile, LANES)]
+    exps = sums[:, pl.ds(rows + tile, LANES)]
+    row = jnp.log(exps) - total[:, 2 * rows :] / plain
     loss[...] = pltpu.roll(row, (LANES - first % LANES) % LANES, 1)[:, : loss.shape[1]]
-    every = (LOSS_SCALE / 0.1) / sums[:, : 2 * rows]
-    for k in range(out.shape[0]):
-        out[k] = every
 
 
 def grad_kernel(
-    order, where, mine, other, units, weight, inverse, scale, factors, out,
-    held, logits, wsub, csub, turned, grad, sems, wsem,
+    order, where, mine, other, units, weight, inverse, scale, factors, own, out, loss,
+    held, logits, wsub, punit, csub, turned, grad, sems, wsem, lsem,
 ):
     core, place = where[0], where[1]
+    lcopy = pltpu.make_async_copy(own, loss, lsem)
+    lcopy.start()
     groups = factors.shape[0]
     rows = factors.shape[2] // 2
     width = wsub.shape[1]
@@ -240,6 +239,7 @@
         copies[-1].start()
     wcopy = pltpu.make_async_copy(weight.at[:, pl.ds(begin, width)], wsub, wsem)
     wcopy.start()
+    punit[...] = jnp.transpose(units[:D, pl.ds(begin, width)])
     inv = inverse[:, pl.ds(begin, width)]
     tiles = width // LANES
     for t in range(tiles):
@@ -254,7 +254,7 @@
     def products(c):
         for k in range(2):
             logits[c % 2, k] = lax.dot_general(
-                units[...], crops_of(c, slice(k * D, (k + 1) * D)), nt, preferred_element_type=F32
+                punit[...], crops_of(c, slice(k * D, (k + 1) * D)), nt, preferred_element_type=F32
             )
 
     products(0)
@@ -295,6 +295,7 @@
     for d in range(0, D, 8):
         cu = wsub[d : d + 8, :] * inv
         out[d // share, d % share : d % share + 8, :] = (grad[d : d + 8, :] - cu * inner) * inv
+    lcopy.wait()
 
 
 def struct(shape, dtype=F32):
@@ -315,14 +316,23 @@
     first = first_crop(number, half, own)
     where = jnp.stack([number & 1, place, first]).astype(jnp.int32)
     swap = [(j, j ^ 1) for j in range(protos)]
-    same_core = [[j for j in range(protos) if j % 2 == core] for core in range(2)]
+    group = [
+        [
+            (2 * y + (pair ^ (j >= protos // 2))) * protos + j
+            for j in range(protos)
+        ]
+        for y in range(crops // 2)
+        for pair in range(2)
+    ]
+    same_core = [g[core::2] for g in group for core in range(2)]
+    both = ("crops", "protos")
     ring = list(range(0, crops, 2)) + list(range(crops - 1, 0, -2))
 
     def over_crops(x):
         return lax.all_to_all(x, "crops", 0, 0, tiled=True)
 
-    def over_protos(x):
-        return lax.all_to_all(x, "protos", 0, 0, tiled=True)
+    def over_group(x):
+        return lax.all_to_all(x, both, 0, 0, tiled=True, axis_index_groups=group)
 
     copies = pl.pallas_call(
         own_kernel,
@@ -334,23 +344,22 @@
         cost_estimate=cost(rows * D, 2 * rows * D),
     )(in_hbm(teacher_feats), in_hbm(student_feats))
     mine = lax.all_to_all(
-        copies, "protos", 0, 0, tiled=True, axis_index_groups=same_core
+        copies, both, 0, 0, tiled=True, axis_index_groups=same_core
     ).reshape(half, 2 * D)
 
-    units, inverse, share_units = pl.pallas_call(
+    units, inverse = pl.pallas_call(
         prep_kernel,
         out_shape=(
-            pltpu.VMEM((D, cols), BF16),
+            pltpu.VMEM((D + SPARE, cols), BF16),
             pltpu.VMEM((1, cols), F32),
-            pltpu.VMEM((width, D), BF16),
         ),
-        in_specs=[SMEM, HBM],
-        out_specs=(VMEM, VMEM, VMEM),
+        in_specs=[HBM],
+        out_specs=(VMEM, VMEM),
         scratch_shapes=[pltpu.VMEM((8, D, cols // 8), F32), pltpu.SemaphoreType.DMA((8,))],
         compiler_params=params(),
         cost_estimate=cost(3 * D * cols, 4 * D * cols),
-    )(where, in_hbm(proto_weight))
-    mine, inverse = lax.optimization_barrier((mine, inverse))
+    )(in_hbm(proto_weight))
+    mine, inverse, where = lax.optimization_barrier((mine, inverse, where))
     other = lax.ppermute(mine, "protos", swap)
     all_mine = lax.all_gather(mine, "crops", axis=0, tiled=True, axis_index_groups=[ring])
 
@@ -400,7 +409,7 @@
             scratch_shapes=[pltpu.VMEM((rows, LANES), F32), pltpu.VMEM((ctile, LANES), F32)],
             compiler_params=params(),
             cost_estimate=cost(2 * rows * cols),
-        )(pinned(table), over_protos(rparts))
+        )(pinned(table), over_group(rparts))
 
     rparts, scale = pl.pallas_call(
         last_kernel,
@@ -414,34 +423,36 @@
     all_mine, rparts = lax.optimization_barrier((all_mine, rparts))
     all_other = lax.ppermute(all_mine, "protos", swap)
     factors, loss = pl.pallas_call(
-        loss_kernel,
-        out_shape=(pltpu.VMEM((crops, 1, 2 * rows), F32), struct((1, own))),
+        factor_kernel,
+        out_shape=(pltpu.VMEM((crops, 1, 2 * rows), F32), pltpu.VMEM((1, own), F32)),
         in_specs=[SMEM, VMEM],
         out_specs=(VMEM, VMEM),
         scratch_shapes=[pltpu.VMEM((1, 2 * rows + LANES), F32)],
         compiler_params=params(),
-    )(where, over_protos(rparts))
-
-    grad = pl.pallas_call(
+    )(where, over_group(rparts))
+
+    grad, loss = pl.pallas_call(
         functools.partial(grad_kernel, ring),
-        out_shape=pltpu.VMEM((crops, share, width), F32),
-        in_specs=[SMEM, HBM, VMEM, VMEM, HBM, VMEM, VMEM, VMEM],
-        out_specs=VMEM,
+        out_shape=(pltpu.VMEM((crops, share, width), F32), pltpu.HBM((1, own), F32)),
+        in_specs=[SMEM, HBM, VMEM, VMEM, HBM, VMEM, VMEM, VMEM, VMEM],
+        out_specs=(VMEM, HBM),
         scratch_shapes=[
             pltpu.VMEM((crops * half, 2 * D), BF16),
             pltpu.VMEM((2, 2, width, half), F32),
             pltpu.VMEM((D, width), F32),
+            pltpu.VMEM((width, D), BF16),
             pltpu.VMEM((width, LANES), F32),
             pltpu.VMEM((width, D), F32),
             pltpu.VMEM((D, width), F32),
             pltpu.SemaphoreType.DMA((crops,)),
             pltpu.SemaphoreType.DMA,
+            pltpu.SemaphoreType.DMA,
         ],
         compiler_params=params(20),
         cost_estimate=cost(6 * CROPS * D * width, 0, 2 * CROPS * width),
     )(
-        where, in_hbm(all_mine), pinned(all_other), pinned(share_units), in_hbm(proto_weight),
-        pinned(inverse), scale, over_crops(factors),
+        where, in_hbm(all_mine), pinned(all_other), pinned(units), in_hbm(proto_weight),
+        pinned(inverse), scale, over_crops(factors), pinned(loss),
     )
     moved = over_crops(grad)
     weight_grad = moved.transpose(1, 0, 2).reshape(share, cols)

time: 163 us -> 160 us (0.982)
  local copies, waits for them, and re-layouts: 2.7 us -> 0.94 us
    all_to_all x5, blocking collectives: 54.3 us -> 58.2 us  [over_crops(): return lax.all_to_all(x, 'crops', 0, 0, tiled=True)]
    all_to_all x3, blocking collectives: 44.2 us -> 40.4 us  [over_group(): return lax.all_to_all(x, both, 0, 0, tiled=True, axis_index_groups=group)]
    unnamed x4 -> x0, local copies, waits for them, and re-layouts: 1.75 us -> none
  transfers between devices with their start and end apart: 4 -> 4, of which waited for: 1 -> 1; matrix products, arithmetic and copies ran while one was open for 0% -> 0% of each run, Pallas kernels for 11% -> 10%
where the time goes in v3:
time: 160 us; the launch traced here: 159 us
  blocking collectives  98.7 us (62%)
  Pallas kernels  26 us (16%)
  between operations  14.1 us (9%)
  starting transfers between devices  9.96 us (6%)
  waiting for transfers between devices  9.58 us (6%)
    all_to_all x5, blocking collectives, over_crops(): return lax.all_to_all(x, 'crops', 0, 0, tiled=True)  58.2 us
    all_to_all x3, blocking collectives, over_group(): return lax.all_to_all(x, both, 0, 0, tiled=True, axis_index_groups=group)  40.4 us
    all_to_all x1, starting transfers between devices, local(): lax.all_to_all(copies, both, 0, 0, tiled=True, axis_index_groups=same_core)  9.55 us
    all_to_all x1, waiting for transfers between devices, local(): lax.all_to_all(copies, both, 0, 0, tiled=True, axis_index_groups=same_core)  9.54 us
    pallas_call x1, Pallas kernels, local(): pl.pallas_call(functools.partial(grad_kernel, ring), out_shape=(pltpu.VME...  8.03 us
    pallas_call x1, Pallas kernels, local(): pl.pallas_call(last_kernel, out_shape=(struct((protos, 1, 2 * rows + LANE...  3.82 us
  transfers between devices with their start and end apart: 4, of which 1 were waited for; matrix products, arithmetic and copies ran while one was open for 0% of the time, Pallas kernels for 10%

profile of v3, /device:TPU:2, one launch (start us, length us, event | category | flops | bytes accessed | tf_op | source)
XLA Modules:
  0.0 159.4 jit_solution(10794008823092022889)
XLA Ops:
  7.2 1.6 %shard_map.50 = bf16[16,16,768]{2,1,0:T(8,128)(2,1)} custom-call(bf16[16,384]{1,0:T(8,128)(2,1)} %teacher.1, bf16[16,384]{1,0:T(8,128)(2,1)} %student.1), custom_call_target="tpu_custom_call" | custom-call | flops 196608 | bytes 393216 | tf_op jit(solution)/shard_map/pallas_call | solution.py:337
  8.8 9.6 %all-to-all-start = ((bf16[16,16,768]{2,1,0:T(8,128)(2,1)}), bf16[16,16,768]{2,1,0:T(8,128)(2,1)}, u32[]{:S(2)}, u32[]{:S(2)}) async-start(bf16[16,16,768]{2,1,0:T(8,128)(2,1)} %shard_map.50), calls=%async_computation | async-start | bytes 786432 | tf_op jit(solution)/shard_map/all_to_all | solution.py:346
  18.3 0.0 all-gather.2.cloned.1.call-start
  18.4 3.0 %shard_map.51 = (bf16[400,4096]{1,0:T(8,128)(2,1)S(1)}, f32[1,4096]{1,0:T(1,128)S(1)}) custom-call(f32[384,4096]{1,0:T(8,128)} %weight.3), custom_call_target="tpu_custom_call" | custom-call | flops 4718592 | bytes 6291456 | tf_op jit(solution)/shard_map/pallas_call | solution.py:350
  21.4 0.1 pad_add_fusion.where
  21.5 9.5 %all-to-all-done = bf16[16,16,768]{2,1,0:T(8,128)(2,1)} async-done(((bf16[16,16,768]{2,1,0:T(8,128)(2,1)}), bf16[16,16,768]{2,1,0:T(8,128)(2,1)}, u32[]{:S(2)}, u32[]{:S(2)}) %all-to-all-start) | async-done | bytes 393248 | tf_op jit(solution)/shard_map/all_to_all | solution.py:346
  31.0 0.0 all-gather.2.cloned.1.call-update
  31.0 0.1 collective-permute-start
  31.1 2.8 %shard_map.52 = (f32[512,4096]{1,0:T(8,128)S(1)}, bf16[512,384]{1,0:T(8,128)(2,1)S(1)}, f32[32,128]{1,0:T(8,128)S(1)}) custom-call(s32[3]{0:T(128)S(1)} %pad_add_fusion.where, bf16[256,768]{1,0:T(8,128)(2,1)} %bitcast.mine, bf16[400,4096]{1,0:T(8,128)(2,1)S(1)} %get-tuple-element.26.units), custom_call_target="tpu_custom_call" | custom-call | flops 805306368 | tf_op jit(solution)/shard_map/pallas_call | solution.py:366
  34.0 0.0 collective-permute-done.other
  34.0 1.8 %shard_map.53 = (f32[512,4096]{1,0:T(8,128)S(1)}, bf16[512,384]{1,0:T(8,128)(2,1)S(1)}, f32[8,32,128]{2,1,0:T(8,128)S(1)}) custom-call(s32[3]{0:T(128)S(1)} %pad_add_fusion.where, bf16[256,768]{1,0:T(8,128)(2,1)S(1)} %collective-permute-done.other, bf16[400,4096]{1,0:T(8,128)(2,1)S(1)} %get-tuple-element.26.units, ...), custom_call_target="tpu_custom_call", output_to_operand_aliasing={{0}: (4, {}), {1}: (5, {})} | custom-call | flops 805306368 | tf_op jit(solution)/shard_map/pallas_call | solution.py:379
  35.8 13.6 %all_to_all.45.parts = f32[8,32,128]{2,1,0:T(8,128)S(1)} all-to-all(f32[8,32,128]{2,1,0:T(8,128)S(1)} %get-tuple-element.31), channel_id=1, replica_groups=mesh['crops'=8,'protos'=32] {'crops'}, dimensions={0} | all-to-all | bytes 262144 | tf_op jit(solution)/shard_map/all_to_all | solution.py:332
  49.4 1.4 shard_map.54
  50.7 14.6 %all_to_all.46.parts = f32[32,4,128]{2,1,0:T(4,128)S(1)} all-to-all(f32[32,4,128]{2,1,0:T(4,128)S(1)} %get-tuple-element.32), channel_id=1, replica_groups={{0,1,2,3,4,5,6,7,8,9,10,11,12,13,14,15,48,49,50,51,52,53,54,55,56,57,58..., dimensions={0} | all-to-all | bytes 131072 | tf_op jit(solution)/shard_map/all_to_all | solution.py:335
  65.3 0.8 shard_map.55
  66.1 10.6 %all_to_all.47.parts = f32[8,32,128]{2,1,0:T(8,128)S(1)} all-to-all(f32[8,32,128]{2,1,0:T(8,128)S(1)} %shard_map.55), channel_id=1, replica_groups=mesh['crops'=8,'protos'=32] {'crops'}, dimensions={0} | all-to-all | bytes 262144 | tf_op jit(solution)/shard_map/all_to_all | solution.py:332
  76.8 1.4 shard_map.56
  78.1 12.0 %all_to_all.48.parts = f32[32,4,128]{2,1,0:T(4,128)S(1)} all-to-all(f32[32,4,128]{2,1,0:T(4,128)S(1)} %get-tuple-element.33), channel_id=1, replica_groups={{0,1,2,3,4,5,6,7,8,9,10,11,12,13,14,15,48,49,50,51,52,53,54,55,56,57,58..., dimensions={0} | all-to-all | bytes 131072 | tf_op jit(solution)/shard_map/all_to_all | solution.py:335
  90.1 0.8 shard_map.57
  90.9 10.7 %all_to_all.49.parts = f32[8,32,128]{2,1,0:T(8,128)S(1)} all-to-all(f32[8,32,128]{2,1,0:T(8,128)S(1)} %shard_map.57), channel_id=1, replica_groups=mesh['crops'=8,'protos'=32] {'crops'}, dimensions={0} | all-to-all | bytes 262144 | tf_op jit(solution)/shard_map/all_to_all | solution.py:332
  101.6 3.8 %shard_map.58 = (f32[32,1,1152]{2,1,0:T(1,128)S(1)}, f32[32,128]{1,0:T(8,128)S(1)}) custom-call(f32[512,4096]{1,0:T(8,128)S(1)} %get-tuple-element.30.table, f32[8,32,128]{2,1,0:T(8,128)S(1)} %all_to_all.49.parts, bf16[512,384]{1,0:T(8,128)(2,1)S(1)} %get-tuple-element.34.student, bf16[400,4096]{1,0:T(8,128)(2,1)S(1)} %get-tuple-element.26.units), custom_call_target="tpu_custom_call" | custom-call | flops 1610612736 | tf_op jit(solution)/shard_map/pallas_call | solution.py:414
  105.5 0.0 all-gather.2.cloned.1.call-done.mine
  105.5 0.3 collective-permute-start.1
  105.8 13.8 %all_to_all.50.parts = f32[32,1,1152]{2,1,0:T(1,128)S(1)} all-to-all(f32[32,1,1152]{2,1,0:T(1,128)S(1)} %get-tuple-element.39), channel_id=1, replica_groups={{0,1,2,3,4,5,6,7,8,9,10,11,12,13,14,15,48,49,50,51,52,53,54,55,56,57,58..., dimensions={0} | all-to-all | bytes 294912 | tf_op jit(solution)/shard_map/all_to_all | solution.py:335
  119.6 0.7 shard_map.59
  120.2 9.7 %all_to_all.51.factors = f32[8,1,1024]{2,1,0:T(1,128)S(1)} all-to-all(f32[8,1,1024]{2,1,0:T(1,128)S(1)} %get-tuple-element.40), channel_id=1, replica_groups=mesh['crops'=8,'protos'=32] {'crops'}, dimensions={0} | all-to-all | bytes 65536 | tf_op jit(solution)/shard_map/all_to_all | solution.py:332
  129.9 0.0 collective-permute-done.1.other
  130.0 8.0 %shard_map.60 = (f32[8,48,512]{2,1,0:T(8,128)S(1)}, f32[1,16]{1,0:T(1,128)}) custom-call(s32[3]{0:T(128)S(1)} %pad_add_fusion.where, bf16[2048,768]{1,0:T(8,128)(2,1)} %all-gather.2.cloned.1.call-done.mine, bf16[2048,768]{1,0:T(8,128)(2,1)S(1)} %collective-permute-done.1.other, bf16[400,4096]{1,0:T(8,128)(2,1)S(1)} %get-tuple-element.26.units, ...), custom_call_target="tpu_custom_call" | custom-call | flops 4831838208 | tf_op jit(solution)/shard_map/pallas_call | solution.py:434
  138.0 13.6 %all_to_all.52 = f32[8,48,512]{2,1,0:T(8,128)S(1)} all-to-all(f32[8,48,512]{2,1,0:T(8,128)S(1)} %get-tuple-element.42), channel_id=1, replica_groups=mesh['crops'=8,'protos'=32] {'crops'}, dimensions={0} | all-to-all | bytes 1572864 | tf_op jit(solution)/shard_map/all_to_all | solution.py:332
  151.6 0.9 copy.8
Async XLA Ops:
  8.8 22.2 %all-to-all-start = ((bf16[16,16,768]{2,1,0:T(8,128)(2,1)}), bf16[16,16,768]{2,1,0:T(8,128)(2,1)}, u32[]{:S(2)}, u32[]{:S(2)}) async-start(bf16[16,16,768]{2,1,0:T(8,128)(2,1)} %shard_map.50), calls=%async_computation | async-start | bytes 786432 | tf_op jit(solution)/shard_map/all_to_all | solution.py:346
  18.3 87.2 %all-gather.2.cloned.1.call-start = ((), (), s32[]{:S(2)}) async-start(), calls=%async_computation.9 | async-start | bytes 3538944 | tf_op jit(solution)/shard_map/all_gather | solution.py:364
  31.0 2.9 %collective-permute-start = (bf16[256,768]{1,0:T(8,128)(2,1)}, bf16[256,768]{1,0:T(8,128)(2,1)S(1)}, u32[]{:S(2)}, u32[]{:S(2)}) collective-permute-start(bf16[256,768]{1,0:T(8,128)(2,1)} %bitcast.mine), channel_id=1, source_target_pairs={{0,1},{1,0},{2,3},{3,2},{4,5},{5,4},{6,7},{7,6},{8,9},{9,8},{10,11... | collective-permute-start | bytes 1179656 | tf_op jit(solution)/shard_map/ppermute | solution.py:363
  105.5 24.4 %collective-permute-start.1 = (bf16[2048,768]{1,0:T(8,128)(2,1)}, bf16[2048,768]{1,0:T(8,128)(2,1)S(1)}, u32[]{:S(2)}, u32[]{:S(2)}) collective-permute-start(bf16[2048,768]{1,0:T(8,128)(2,1)} %all-gather.2.cloned.1.call-done.mine), channel_id=1, source_target_pairs={{0,1},{1,0},{2,3},{3,2},{4,5},{5,4},{6,7},{7,6},{8,9},{9,8},{10,11... | collective-permute-start | bytes 9437192 | tf_op jit(solution)/shard_map/ppermute | solution.py:424
Sparse Core Ops, SparseCore 0:
  31.1 45.1 all-gather.1

commit v4 on v3

--- a/solution.py
+++ b/solution.py
@@ -84,9 +84,8 @@
         total[start + t : start + t + 1, :] = sums[:, t * LANES : (t + 1) * LANES]
 
 
-def exp_rows(rows, start, units, table, student, total):
+def exp_rows(rows, start, units, table, total):
     half = rows.shape[0]
-    student[pl.ds(start, half), :] = rows[:, D:]
     width = 512
     for k in range(table.shape[1] // width):
         cols = slice(k * width, (k + 1) * width)
@@ -98,17 +97,27 @@
         col_rows(total, jnp.sum(sums, axis=0, keepdims=True), k * width // LANES)
 
 
-def exp_mine_kernel(where, mine, units, table, student, total, held, sem):
-    copy = pltpu.make_async_copy(mine, held, sem)
-    copy.start()
-    copy.wait()
+def exp_mine_kernel(where, mine, units, table, student, total, held, sems):
     half = held.shape[0]
-    exp_rows(held, pl.multiple_of(where[0] * half, half), units, table, student, total)
+    start = pl.multiple_of(where[0] * half, half)
+    copies = [
+        pltpu.make_async_copy(mine.at[:, pl.ds(0, D)], held, sems.at[0]),
+        pltpu.make_async_copy(
+            mine.at[:, pl.ds(D, D)], student.at[pl.ds(start, half), :], sems.at[1]
+        ),
+    ]
+    for copy in copies:
+        copy.start()
+    copies[0].wait()
+    exp_rows(held, start, units, table, total)
+    copies[1].wait()
 
 
 def exp_other_kernel(where, other, units, first, _, __, table, student, out, total):
     half = other.shape[0]
-    exp_rows(other, pl.multiple_of((1 - where[0]) * half, half), units, table, student, total)
+    start = pl.multiple_of((1 - where[0]) * half, half)
+    student[pl.ds(start, half), :] = other[:, D:]
+    exp_rows(other, start, units, table, total)
     every = first[...] + total[...]
     for k in range(out.shape[0]):
         out[k] = every
@@ -372,7 +381,7 @@
         ),
         in_specs=[SMEM, HBM, VMEM],
         out_specs=(VMEM, VMEM, VMEM),
-        scratch_shapes=[pltpu.VMEM((half, 2 * D), BF16), pltpu.SemaphoreType.DMA],
+        scratch_shapes=[pltpu.VMEM((half, D), BF16), pltpu.SemaphoreType.DMA((2,))],
         compiler_params=params(),
         cost_estimate=cost(rows * D * cols, 0, rows * cols // 2),
     )(where, in_hbm(mine), pinned(units))

time: 160 us -> 160 us (level)
  no operation moved by 1% of the time
where the time goes in v4:
time: 160 us; the launch traced here: 159 us
  blocking collectives  98.7 us (62%)
  Pallas kernels  26 us (16%)
  between operations  14.1 us (9%)
  starting transfers between devices  9.96 us (6%)
  waiting for transfers between devices  9.58 us (6%)
    all_to_all x5, blocking collectives, over_crops(): return lax.all_to_all(x, 'crops', 0, 0, tiled=True)  58.3 us
    all_to_all x3, blocking collectives, over_group(): return lax.all_to_all(x, both, 0, 0, tiled=True, axis_index_groups=group)  40.4 us
    all_to_all x1, starting transfers between devices, local(): lax.all_to_all(copies, both, 0, 0, tiled=True, axis_index_groups=same_core)  9.55 us
    all_to_all x1, waiting for transfers between devices, local(): lax.all_to_all(copies, both, 0, 0, tiled=True, axis_index_groups=same_core)  9.54 us
    pallas_call x1, Pallas kernels, local(): pl.pallas_call(functools.partial(grad_kernel, ring), out_shape=(pltpu.VME...  8.03 us
    pallas_call x1, Pallas kernels, local(): pl.pallas_call(last_kernel, out_shape=(struct((protos, 1, 2 * rows + LANE...  3.82 us
  transfers between devices with their start and end apart: 4, of which 1 were waited for; matrix products, arithmetic and copies ran while one was open for 0% of the time, Pallas kernels for 10%

profile of v4, /device:TPU:2, one launch (start us, length us, event | category | flops | bytes accessed | tf_op | source)
XLA Modules:
  0.0 159.4 jit_solution(5348525431691069577)
XLA Ops:
  7.2 1.6 %shard_map.50 = bf16[16,16,768]{2,1,0:T(8,128)(2,1)} custom-call(bf16[16,384]{1,0:T(8,128)(2,1)} %teacher.1, bf16[16,384]{1,0:T(8,128)(2,1)} %student.1), custom_call_target="tpu_custom_call" | custom-call | flops 196608 | bytes 393216 | tf_op jit(solution)/shard_map/pallas_call | solution.py:346
  8.8 9.6 %all-to-all-start = ((bf16[16,16,768]{2,1,0:T(8,128)(2,1)}), bf16[16,16,768]{2,1,0:T(8,128)(2,1)}, u32[]{:S(2)}, u32[]{:S(2)}) async-start(bf16[16,16,768]{2,1,0:T(8,128)(2,1)} %shard_map.50), calls=%async_computation | async-start | bytes 786432 | tf_op jit(solution)/shard_map/all_to_all | solution.py:355
  18.3 0.0 all-gather.2.cloned.1.call-start
  18.4 3.0 %shard_map.51 = (bf16[400,4096]{1,0:T(8,128)(2,1)S(1)}, f32[1,4096]{1,0:T(1,128)S(1)}) custom-call(f32[384,4096]{1,0:T(8,128)} %weight.3), custom_call_target="tpu_custom_call" | custom-call | flops 4718592 | bytes 6291456 | tf_op jit(solution)/shard_map/pallas_call | solution.py:359
  21.4 0.1 pad_add_fusion.where
  21.5 9.5 %all-to-all-done = bf16[16,16,768]{2,1,0:T(8,128)(2,1)} async-done(((bf16[16,16,768]{2,1,0:T(8,128)(2,1)}), bf16[16,16,768]{2,1,0:T(8,128)(2,1)}, u32[]{:S(2)}, u32[]{:S(2)}) %all-to-all-start) | async-done | bytes 393248 | tf_op jit(solution)/shard_map/all_to_all | solution.py:355
  31.0 0.0 all-gather.2.cloned.1.call-update
  31.0 0.1 collective-permute-start
  31.1 2.8 %shard_map.52 = (f32[512,4096]{1,0:T(8,128)S(1)}, bf16[512,384]{1,0:T(8,128)(2,1)S(1)}, f32[32,128]{1,0:T(8,128)S(1)}) custom-call(s32[3]{0:T(128)S(1)} %pad_add_fusion.where, bf16[256,768]{1,0:T(8,128)(2,1)} %bitcast.mine, bf16[400,4096]{1,0:T(8,128)(2,1)S(1)} %get-tuple-element.26.units), custom_call_target="tpu_custom_call" | custom-call | flops 805306368 | tf_op jit(solution)/shard_map/pallas_call | solution.py:375
  33.9 0.0 collective-permute-done.other
  33.9 1.8 %shard_map.53 = (f32[512,4096]{1,0:T(8,128)S(1)}, bf16[512,384]{1,0:T(8,128)(2,1)S(1)}, f32[8,32,128]{2,1,0:T(8,128)S(1)}) custom-call(s32[3]{0:T(128)S(1)} %pad_add_fusion.where, bf16[256,768]{1,0:T(8,128)(2,1)S(1)} %collective-permute-done.other, bf16[400,4096]{1,0:T(8,128)(2,1)S(1)} %get-tuple-element.26.units, ...), custom_call_target="tpu_custom_call", output_to_operand_aliasing={{0}: (4, {}), {1}: (5, {})} | custom-call | flops 805306368 | tf_op jit(solution)/shard_map/pallas_call | solution.py:388
  35.7 13.6 %all_to_all.45.parts = f32[8,32,128]{2,1,0:T(8,128)S(1)} all-to-all(f32[8,32,128]{2,1,0:T(8,128)S(1)} %get-tuple-element.31), channel_id=1, replica_groups=mesh['crops'=8,'protos'=32] {'crops'}, dimensions={0} | all-to-all | bytes 262144 | tf_op jit(solution)/shard_map/all_to_all | solution.py:341
  49.3 1.4 shard_map.54
  50.6 14.6 %all_to_all.46.parts = f32[32,4,128]{2,1,0:T(4,128)S(1)} all-to-all(f32[32,4,128]{2,1,0:T(4,128)S(1)} %get-tuple-element.32), channel_id=1, replica_groups={{0,1,2,3,4,5,6,7,8,9,10,11,12,13,14,15,48,49,50,51,52,53,54,55,56,57,58..., dimensions={0} | all-to-all | bytes 131072 | tf_op jit(solution)/shard_map/all_to_all | solution.py:344
  65.3 0.8 shard_map.55
  66.1 10.6 %all_to_all.47.parts = f32[8,32,128]{2,1,0:T(8,128)S(1)} all-to-all(f32[8,32,128]{2,1,0:T(8,128)S(1)} %shard_map.55), channel_id=1, replica_groups=mesh['crops'=8,'protos'=32] {'crops'}, dimensions={0} | all-to-all | bytes 262144 | tf_op jit(solution)/shard_map/all_to_all | solution.py:341
  76.7 1.4 shard_map.56
  78.0 12.0 %all_to_all.48.parts = f32[32,4,128]{2,1,0:T(4,128)S(1)} all-to-all(f32[32,4,128]{2,1,0:T(4,128)S(1)} %get-tuple-element.33), channel_id=1, replica_groups={{0,1,2,3,4,5,6,7,8,9,10,11,12,13,14,15,48,49,50,51,52,53,54,55,56,57,58..., dimensions={0} | all-to-all | bytes 131072 | tf_op jit(solution)/shard_map/all_to_all | solution.py:344
  90.1 0.8 shard_map.57
  90.9 10.8 %all_to_all.49.parts = f32[8,32,128]{2,1,0:T(8,128)S(1)} all-to-all(f32[8,32,128]{2,1,0:T(8,128)S(1)} %shard_map.57), channel_id=1, replica_groups=mesh['crops'=8,'protos'=32] {'crops'}, dimensions={0} | all-to-all | bytes 262144 | tf_op jit(solution)/shard_map/all_to_all | solution.py:341
  101.6 3.8 %shard_map.58 = (f32[32,1,1152]{2,1,0:T(1,128)S(1)}, f32[32,128]{1,0:T(8,128)S(1)}) custom-call(f32[512,4096]{1,0:T(8,128)S(1)} %get-tuple-element.30.table, f32[8,32,128]{2,1,0:T(8,128)S(1)} %all_to_all.49.parts, bf16[512,384]{1,0:T(8,128)(2,1)S(1)} %get-tuple-element.34.student, bf16[400,4096]{1,0:T(8,128)(2,1)S(1)} %get-tuple-element.26.units), custom_call_target="tpu_custom_call" | custom-call | flops 1610612736 | tf_op jit(solution)/shard_map/pallas_call | solution.py:423
  105.5 0.0 all-gather.2.cloned.1.call-done.mine
  105.5 0.3 collective-permute-start.1
  105.8 13.8 %all_to_all.50.parts = f32[32,1,1152]{2,1,0:T(1,128)S(1)} all-to-all(f32[32,1,1152]{2,1,0:T(1,128)S(1)} %get-tuple-element.39), channel_id=1, replica_groups={{0,1,2,3,4,5,6,7,8,9,10,11,12,13,14,15,48,49,50,51,52,53,54,55,56,57,58..., dimensions={0} | all-to-all | bytes 294912 | tf_op jit(solution)/shard_map/all_to_all | solution.py:344
  119.5 0.7 shard_map.59
  120.2 9.7 %all_to_all.51.factors = f32[8,1,1024]{2,1,0:T(1,128)S(1)} all-to-all(f32[8,1,1024]{2,1,0:T(1,128)S(1)} %get-tuple-element.40), channel_id=1, replica_groups=mesh['crops'=8,'protos'=32] {'crops'}, dimensions={0} | all-to-all | bytes 65536 | tf_op jit(solution)/shard_map/all_to_all | solution.py:341
  130.0 0.0 collective-permute-done.1.other
  130.0 8.0 %shard_map.60 = (f32[8,48,512]{2,1,0:T(8,128)S(1)}, f32[1,16]{1,0:T(1,128)}) custom-call(s32[3]{0:T(128)S(1)} %pad_add_fusion.where, bf16[2048,768]{1,0:T(8,128)(2,1)} %all-gather.2.cloned.1.call-done.mine, bf16[2048,768]{1,0:T(8,128)(2,1)S(1)} %collective-permute-done.1.other, bf16[400,4096]{1,0:T(8,128)(2,1)S(1)} %get-tuple-element.26.units, ...), custom_call_target="tpu_custom_call" | custom-call | flops 4831838208 | tf_op jit(solution)/shard_map/pallas_call | solution.py:443
  138.0 13.6 %all_to_all.52 = f32[8,48,512]{2,1,0:T(8,128)S(1)} all-to-all(f32[8,48,512]{2,1,0:T(8,128)S(1)} %get-tuple-element.42), channel_id=1, replica_groups=mesh['crops'=8,'protos'=32] {'crops'}, dimensions={0} | all-to-all | bytes 1572864 | tf_op jit(solution)/shard_map/all_to_all | solution.py:341
  151.6 0.9 copy.8
Async XLA Ops:
  8.8 22.2 %all-to-all-start = ((bf16[16,16,768]{2,1,0:T(8,128)(2,1)}), bf16[16,16,768]{2,1,0:T(8,128)(2,1)}, u32[]{:S(2)}, u32[]{:S(2)}) async-start(bf16[16,16,768]{2,1,0:T(8,128)(2,1)} %shard_map.50), calls=%async_computation | async-start | bytes 786432 | tf_op jit(solution)/shard_map/all_to_all | solution.py:355
  18.3 87.2 %all-gather.2.cloned.1.call-start = ((), (), s32[]{:S(2)}) async-start(), calls=%async_computation.9 | async-start | bytes 3538944 | tf_op jit(solution)/shard_map/all_gather | solution.py:373
  31.0 2.9 %collective-permute-start = (bf16[256,768]{1,0:T(8,128)(2,1)}, bf16[256,768]{1,0:T(8,128)(2,1)S(1)}, u32[]{:S(2)}, u32[]{:S(2)}) collective-permute-start(bf16[256,768]{1,0:T(8,128)(2,1)} %bitcast.mine), channel_id=1, source_target_pairs={{0,1},{1,0},{2,3},{3,2},{4,5},{5,4},{6,7},{7,6},{8,9},{9,8},{10,11... | collective-permute-start | bytes 1179656 | tf_op jit(solution)/shard_map/ppermute | solution.py:372
  105.5 24.5 %collective-permute-start.1 = (bf16[2048,768]{1,0:T(8,128)(2,1)}, bf16[2048,768]{1,0:T(8,128)(2,1)S(1)}, u32[]{:S(2)}, u32[]{:S(2)}) collective-permute-start(bf16[2048,768]{1,0:T(8,128)(2,1)} %all-gather.2.cloned.1.call-done.mine), channel_id=1, source_target_pairs={{0,1},{1,0},{2,3},{3,2},{4,5},{5,4},{6,7},{7,6},{8,9},{9,8},{10,11... | collective-permute-start | bytes 9437192 | tf_op jit(solution)/shard_map/ppermute | solution.py:433
Sparse Core Ops, SparseCore 0:
  31.1 45.1 all-gather.1

commit v5 on v4

--- a/solution.py
+++ b/solution.py
@@ -401,12 +401,16 @@
     )(where, other, pinned(units), pinned(total), pinned(table), pinned(student))
 
     for step in range(2):
-        rparts, _ = pl.pallas_call(
+        rparts = pl.pallas_call(
             row_kernel,
-            out_shape=(struct((protos, rtile, LANES)), struct((ctile, LANES))),
+            out_shape=struct((protos, rtile, LANES)),
             in_specs=[VMEM, VMEM],
-            out_specs=(VMEM, VMEM),
-            scratch_shapes=[pltpu.VMEM((rows, LANES), F32), pltpu.VMEM((rtile, LANES), F32)],
+            out_specs=VMEM,
+            scratch_shapes=[
+                pltpu.VMEM((ctile, LANES), F32),
+                pltpu.VMEM((rows, LANES), F32),
+                pltpu.VMEM((rtile, LANES), F32),
+            ],
             compiler_params=params(),
             cost_estimate=cost(2 * rows * cols),
         )(pinned(table), over_crops(parts))

time: 160 us -> 160 us (level)
  no operation moved by 1% of the time
where the time goes in v5:
time: 160 us; the launch traced here: 159 us
  blocking collectives  98.9 us (62%)
  Pallas kernels  25.5 us (16%)
  between operations  14.1 us (9%)
  starting transfers between devices  9.96 us (6%)
  waiting for transfers between devices  9.58 us (6%)
    all_to_all x5, blocking collectives, over_crops(): return lax.all_to_all(x, 'crops', 0, 0, tiled=True)  58.4 us
    all_to_all x3, blocking collectives, over_group(): return lax.all_to_all(x, both, 0, 0, tiled=True, axis_index_groups=group)  40.4 us
    all_to_all x1, starting transfers between devices, local(): lax.all_to_all(copies, both, 0, 0, tiled=True, axis_index_groups=same_core)  9.55 us
    all_to_all x1, waiting for transfers between devices, local(): lax.all_to_all(copies, both, 0, 0, tiled=True, axis_index_groups=same_core)  9.54 us
    pallas_call x1, Pallas kernels, local(): pl.pallas_call(functools.partial(grad_kernel, ring), out_shape=(pltpu.VME...  8.03 us
    pallas_call x1, Pallas kernels, local(): pl.pallas_call(last_kernel, out_shape=(struct((protos, 1, 2 * rows + LANE...  3.82 us
  transfers between devices with their start and end apart: 4, of which 1 were waited for; matrix products, arithmetic and copies ran while one was open for 0% of the time, Pallas kernels for 10%

profile of v5, /device:TPU:2, one launch (start us, length us, event | category | flops | bytes accessed | tf_op | source)
XLA Modules:
  0.0 159.0 jit_solution(7087607139085795137)
XLA Ops:
  7.2 1.6 %shard_map.50 = bf16[16,16,768]{2,1,0:T(8,128)(2,1)} custom-call(bf16[16,384]{1,0:T(8,128)(2,1)} %teacher.1, bf16[16,384]{1,0:T(8,128)(2,1)} %student.1), custom_call_target="tpu_custom_call" | custom-call | flops 196608 | bytes 393216 | tf_op jit(solution)/shard_map/pallas_call | solution.py:346
  8.8 9.6 %all-to-all-start = ((bf16[16,16,768]{2,1,0:T(8,128)(2,1)}), bf16[16,16,768]{2,1,0:T(8,128)(2,1)}, u32[]{:S(2)}, u32[]{:S(2)}) async-start(bf16[16,16,768]{2,1,0:T(8,128)(2,1)} %shard_map.50), calls=%async_computation | async-start | bytes 786432 | tf_op jit(solution)/shard_map/all_to_all | solution.py:355
  18.3 0.0 all-gather.2.cloned.1.call-start
  18.4 3.0 %shard_map.51 = (bf16[400,4096]{1,0:T(8,128)(2,1)S(1)}, f32[1,4096]{1,0:T(1,128)S(1)}) custom-call(f32[384,4096]{1,0:T(8,128)} %weight.3), custom_call_target="tpu_custom_call" | custom-call | flops 4718592 | bytes 6291456 | tf_op jit(solution)/shard_map/pallas_call | solution.py:359
  21.4 0.1 pad_add_fusion.where
  21.5 9.5 %all-to-all-done = bf16[16,16,768]{2,1,0:T(8,128)(2,1)} async-done(((bf16[16,16,768]{2,1,0:T(8,128)(2,1)}), bf16[16,16,768]{2,1,0:T(8,128)(2,1)}, u32[]{:S(2)}, u32[]{:S(2)}) %all-to-all-start) | async-done | bytes 393248 | tf_op jit(solution)/shard_map/all_to_all | solution.py:355
  31.0 0.0 all-gather.2.cloned.1.call-update
  31.0 0.1 collective-permute-start
  31.1 2.8 %shard_map.52 = (f32[512,4096]{1,0:T(8,128)S(1)}, bf16[512,384]{1,0:T(8,128)(2,1)S(1)}, f32[32,128]{1,0:T(8,128)S(1)}) custom-call(s32[3]{0:T(128)S(1)} %pad_add_fusion.where, bf16[256,768]{1,0:T(8,128)(2,1)} %bitcast.mine, bf16[400,4096]{1,0:T(8,128)(2,1)S(1)} %get-tuple-element.24.units), custom_call_target="tpu_custom_call" | custom-call | flops 805306368 | tf_op jit(solution)/shard_map/pallas_call | solution.py:375
  33.9 0.0 collective-permute-done.other
  33.9 1.8 %shard_map.53 = (f32[512,4096]{1,0:T(8,128)S(1)}, bf16[512,384]{1,0:T(8,128)(2,1)S(1)}, f32[8,32,128]{2,1,0:T(8,128)S(1)}) custom-call(s32[3]{0:T(128)S(1)} %pad_add_fusion.where, bf16[256,768]{1,0:T(8,128)(2,1)S(1)} %collective-permute-done.other, bf16[400,4096]{1,0:T(8,128)(2,1)S(1)} %get-tuple-element.24.units, ...), custom_call_target="tpu_custom_call", output_to_operand_aliasing={{0}: (4, {}), {1}: (5, {})} | custom-call | flops 805306368 | tf_op jit(solution)/shard_map/pallas_call | solution.py:388
  35.7 13.6 %all_to_all.45.parts = f32[8,32,128]{2,1,0:T(8,128)S(1)} all-to-all(f32[8,32,128]{2,1,0:T(8,128)S(1)} %get-tuple-element.29), channel_id=1, replica_groups=mesh['crops'=8,'protos'=32] {'crops'}, dimensions={0} | all-to-all | bytes 262144 | tf_op jit(solution)/shard_map/all_to_all | solution.py:341
  49.3 1.1 shard_map.54
  50.4 14.6 %all_to_all.46.parts = f32[32,4,128]{2,1,0:T(4,128)S(1)} all-to-all(f32[32,4,128]{2,1,0:T(4,128)S(1)} %shard_map.54), channel_id=1, replica_groups={{0,1,2,3,4,5,6,7,8,9,10,11,12,13,14,15,48,49,50,51,52,53,54,55,56,57,58..., dimensions={0} | all-to-all | bytes 131072 | tf_op jit(solution)/shard_map/all_to_all | solution.py:344
  65.0 0.8 shard_map.55
  65.8 10.6 %all_to_all.47.parts = f32[8,32,128]{2,1,0:T(8,128)S(1)} all-to-all(f32[8,32,128]{2,1,0:T(8,128)S(1)} %shard_map.55), channel_id=1, replica_groups=mesh['crops'=8,'protos'=32] {'crops'}, dimensions={0} | all-to-all | bytes 262144 | tf_op jit(solution)/shard_map/all_to_all | solution.py:341
  76.5 1.1 shard_map.56
  77.6 12.0 %all_to_all.48.parts = f32[32,4,128]{2,1,0:T(4,128)S(1)} all-to-all(f32[32,4,128]{2,1,0:T(4,128)S(1)} %shard_map.56), channel_id=1, replica_groups={{0,1,2,3,4,5,6,7,8,9,10,11,12,13,14,15,48,49,50,51,52,53,54,55,56,57,58..., dimensions={0} | all-to-all | bytes 131072 | tf_op jit(solution)/shard_map/all_to_all | solution.py:344
  89.6 0.8 shard_map.57
  90.4 10.9 %all_to_all.49.parts = f32[8,32,128]{2,1,0:T(8,128)S(1)} all-to-all(f32[8,32,128]{2,1,0:T(8,128)S(1)} %shard_map.57), channel_id=1, replica_groups=mesh['crops'=8,'protos'=32] {'crops'}, dimensions={0} | all-to-all | bytes 262144 | tf_op jit(solution)/shard_map/all_to_all | solution.py:341
  101.3 3.8 %shard_map.58 = (f32[32,1,1152]{2,1,0:T(1,128)S(1)}, f32[32,128]{1,0:T(8,128)S(1)}) custom-call(f32[512,4096]{1,0:T(8,128)S(1)} %get-tuple-element.28.table, f32[8,32,128]{2,1,0:T(8,128)S(1)} %all_to_all.49.parts, bf16[512,384]{1,0:T(8,128)(2,1)S(1)} %get-tuple-element.30.student, bf16[400,4096]{1,0:T(8,128)(2,1)S(1)} %get-tuple-element.24.units), custom_call_target="tpu_custom_call" | custom-call | flops 1610612736 | tf_op jit(solution)/shard_map/pallas_call | solution.py:427
  105.1 0.0 all-gather.2.cloned.1.call-done.mine
  105.2 0.3 collective-permute-start.1
  105.5 13.8 %all_to_all.50.parts = f32[32,1,1152]{2,1,0:T(1,128)S(1)} all-to-all(f32[32,1,1152]{2,1,0:T(1,128)S(1)} %get-tuple-element.35), channel_id=1, replica_groups={{0,1,2,3,4,5,6,7,8,9,10,11,12,13,14,15,48,49,50,51,52,53,54,55,56,57,58..., dimensions={0} | all-to-all | bytes 294912 | tf_op jit(solution)/shard_map/all_to_all | solution.py:344
  119.2 0.7 shard_map.59
  119.9 9.7 %all_to_all.51.factors = f32[8,1,1024]{2,1,0:T(1,128)S(1)} all-to-all(f32[8,1,1024]{2,1,0:T(1,128)S(1)} %get-tuple-element.36), channel_id=1, replica_groups=mesh['crops'=8,'protos'=32] {'crops'}, dimensions={0} | all-to-all | bytes 65536 | tf_op jit(solution)/shard_map/all_to_all | solution.py:341
  129.6 0.0 collective-permute-done.1.other
  129.6 8.0 %shard_map.60 = (f32[8,48,512]{2,1,0:T(8,128)S(1)}, f32[1,16]{1,0:T(1,128)}) custom-call(s32[3]{0:T(128)S(1)} %pad_add_fusion.where, bf16[2048,768]{1,0:T(8,128)(2,1)} %all-gather.2.cloned.1.call-done.mine, bf16[2048,768]{1,0:T(8,128)(2,1)S(1)} %collective-permute-done.1.other, bf16[400,4096]{1,0:T(8,128)(2,1)S(1)} %get-tuple-element.24.units, ...), custom_call_target="tpu_custom_call" | custom-call | flops 4831838208 | tf_op jit(solution)/shard_map/pallas_call | solution.py:447
  137.7 13.6 %all_to_all.52 = f32[8,48,512]{2,1,0:T(8,128)S(1)} all-to-all(f32[8,48,512]{2,1,0:T(8,128)S(1)} %get-tuple-element.38), channel_id=1, replica_groups=mesh['crops'=8,'protos'=32] {'crops'}, dimensions={0} | all-to-all | bytes 1572864 | tf_op jit(solution)/shard_map/all_to_all | solution.py:341
  151.3 0.9 copy.8
Async XLA Ops:
  8.8 22.2 %all-to-all-start = ((bf16[16,16,768]{2,1,0:T(8,128)(2,1)}), bf16[16,16,768]{2,1,0:T(8,128)(2,1)}, u32[]{:S(2)}, u32[]{:S(2)}) async-start(bf16[16,16,768]{2,1,0:T(8,128)(2,1)} %shard_map.50), calls=%async_computation | async-start | bytes 786432 | tf_op jit(solution)/shard_map/all_to_all | solution.py:355
  18.3 86.8 %all-gather.2.cloned.1.call-start = ((), (), s32[]{:S(2)}) async-start(), calls=%async_computation.9 | async-start | bytes 3538944 | tf_op jit(solution)/shard_map/all_gather | solution.py:373
  31.0 2.9 %collective-permute-start = (bf16[256,768]{1,0:T(8,128)(2,1)}, bf16[256,768]{1,0:T(8,128)(2,1)S(1)}, u32[]{:S(2)}, u32[]{:S(2)}) collective-permute-start(bf16[256,768]{1,0:T(8,128)(2,1)} %bitcast.mine), channel_id=1, source_target_pairs={{0,1},{1,0},{2,3},{3,2},{4,5},{5,4},{6,7},{7,6},{8,9},{9,8},{10,11... | collective-permute-start | bytes 1179656 | tf_op jit(solution)/shard_map/ppermute | solution.py:372
  105.2 24.5 %collective-permute-start.1 = (bf16[2048,768]{1,0:T(8,128)(2,1)}, bf16[2048,768]{1,0:T(8,128)(2,1)S(1)}, u32[]{:S(2)}, u32[]{:S(2)}) collective-permute-start(bf16[2048,768]{1,0:T(8,128)(2,1)} %all-gather.2.cloned.1.call-done.mine), channel_id=1, source_target_pairs={{0,1},{1,0},{2,3},{3,2},{4,5},{5,4},{6,7},{7,6},{8,9},{9,8},{10,11... | collective-permute-start | bytes 9437192 | tf_op jit(solution)/shard_map/ppermute | solution.py:437
Sparse Core Ops, SparseCore 0:
  31.1 45.1 all-gather.1

commit v6 on v5

--- a/solution.py
+++ b/solution.py
@@ -22,7 +22,6 @@
 STUDENT = 1.0 / 0.1
 LOG2E = math.log2(math.e)
 VMEM = pl.BlockSpec(memory_space=pltpu.VMEM)
-SMEM = pl.BlockSpec(memory_space=pltpu.SMEM)
 HBM = pl.BlockSpec(memory_space=pltpu.HBM)
 
 
@@ -97,9 +96,9 @@
         col_rows(total, jnp.sum(sums, axis=0, keepdims=True), k * width // LANES)
 
 
-def exp_mine_kernel(where, mine, units, table, student, total, held, sems):
+def exp_mine_kernel(mine, units, table, student, total, held, sems):
     half = held.shape[0]
-    start = pl.multiple_of(where[0] * half, half)
+    start = pl.multiple_of((lax.axis_index("protos") & 1) * half, half)
     copies = [
         pltpu.make_async_copy(mine.at[:, pl.ds(0, D)], held, sems.at[0]),
         pltpu.make_async_copy(
@@ -113,9 +112,9 @@
     copies[1].wait()
 
 
-def exp_other_kernel(where, other, units, first, _, __, table, student, out, total):
+def exp_other_kernel(other, units, first, _, __, table, student, out, total):
     half = other.shape[0]
-    start = pl.multiple_of((1 - where[0]) * half, half)
+    start = pl.multiple_of((1 - (lax.axis_index("protos") & 1)) * half, half)
     student[pl.ds(start, half), :] = other[:, D:]
     exp_rows(other, start, units, table, total)
     every = first[...] + total[...]
@@ -212,7 +211,7 @@
     return (number & 1) * half + (number >> 1) * own
 
 
-def factor_kernel(where, parts, out, loss, sums):
+def factor_kernel(parts, out, loss, sums):
     total = parts[0]
     for k in range(1, parts.shape[0]):
         total += parts[k]
@@ -221,7 +220,7 @@
     every = (LOSS_SCALE / 0.1) / total[:, : 2 * rows]
     for k in range(out.shape[0]):
         out[k] = every
-    first = where[2]
+    first = first_crop(lax.axis_index("protos"), rows // 2, loss.shape[1])
     tile = pl.multiple_of(first // LANES * LANES, LANES)
     plain = sums[:, pl.ds(tile, LANES)]
     exps = sums[:, pl.ds(rows + tile, LANES)]
@@ -230,10 +229,10 @@
 
 
 def grad_kernel(
-    order, where, mine, other, units, weight, inverse, scale, factors, own, out, loss,
+    order, mine, other, units, weight, inverse, scale, factors, own, out, loss,
     held, logits, wsub, punit, csub, turned, grad, sems, wsem, lsem,
 ):
-    core, place = where[0], where[1]
+    core, place = lax.axis_index("protos") & 1, lax.axis_index("crops")
     lcopy = pltpu.make_async_copy(own, loss, lsem)
     lcopy.start()
     groups = factors.shape[0]
@@ -320,10 +319,6 @@
     width = cols // crops
     share = D // crops
     ctile, rtile = cols // LANES, rows // LANES
-    number = lax.axis_index("protos")
-    place = lax.axis_index("crops")
-    first = first_crop(number, half, own)
-    where = jnp.stack([number & 1, place, first]).astype(jnp.int32)
     swap = [(j, j ^ 1) for j in range(protos)]
     group = [
         [
@@ -368,7 +363,7 @@
         compiler_params=params(),
         cost_estimate=cost(3 * D * cols, 4 * D * cols),
     )(in_hbm(proto_weight))
-    mine, inverse, where = lax.optimization_barrier((mine, inverse, where))
+    mine, inverse = lax.optimization_barrier((mine, inverse))
     other = lax.ppermute(mine, "protos", swap)
     all_mine = lax.all_gather(mine, "crops", axis=0, tiled=True, axis_index_groups=[ring])
 
@@ -379,12 +374,12 @@
             pltpu.VMEM((rows, D), BF16),
             pltpu.VMEM((ctile, LANES), F32),
         ),
-        in_specs=[SMEM, HBM, VMEM],
+        in_specs=[HBM, VMEM],
         out_specs=(VMEM, VMEM, VMEM),
         scratch_shapes=[pltpu.VMEM((half, D), BF16), pltpu.SemaphoreType.DMA((2,))],
         compiler_params=params(),
         cost_estimate=cost(rows * D * cols, 0, rows * cols // 2),
-    )(where, in_hbm(mine), pinned(units))
+    )(in_hbm(mine), pinned(units))
     table, student, parts = pl.pallas_call(
         exp_other_kernel,
         out_shape=(
@@ -392,13 +387,13 @@
             pltpu.VMEM((rows, D), BF16),
             struct((crops, ctile, LANES)),
         ),
-        in_specs=[SMEM] + [VMEM] * 5,
+        in_specs=[VMEM] * 5,
         out_specs=(VMEM, VMEM, VMEM),
-        input_output_aliases={4: 0, 5: 1},
+        input_output_aliases={3: 0, 4: 1},
         scratch_shapes=[pltpu.VMEM((ctile, LANES), F32)],
         compiler_params=params(),
         cost_estimate=cost(rows * D * cols, 0, rows * cols // 2),
-    )(where, other, pinned(units), pinned(total), pinned(table), pinned(student))
+    )(other, pinned(units), pinned(total), pinned(table), pinned(student))
 
     for step in range(2):
         rparts = pl.pallas_call(
@@ -438,16 +433,16 @@
     factors, loss = pl.pallas_call(
         factor_kernel,
         out_shape=(pltpu.VMEM((crops, 1, 2 * rows), F32), pltpu.VMEM((1, own), F32)),
-        in_specs=[SMEM, VMEM],
+        in_specs=[VMEM],
         out_specs=(VMEM, VMEM),
         scratch_shapes=[pltpu.VMEM((1, 2 * rows + LANES), F32)],
         compiler_params=params(),
-    )(where, over_group(rparts))
+    )(over_group(rparts))
 
     grad, loss = pl.pallas_call(
         functools.partial(grad_kernel, ring),
         out_shape=(pltpu.VMEM((crops, share, width), F32), pltpu.HBM((1, own), F32)),
-        in_specs=[SMEM, HBM, VMEM, VMEM, HBM, VMEM, VMEM, VMEM, VMEM],
+        in_specs=[HBM, VMEM, VMEM, HBM, VMEM, VMEM, VMEM, VMEM],
         out_specs=(VMEM, HBM),
         scratch_shapes=[
             pltpu.VMEM((crops * half, 2 * D), BF16),
@@ -464,7 +459,7 @@
         compiler_params=params(20),
         cost_estimate=cost(6 * CROPS * D * width, 0, 2 * CROPS * width),
     )(
-        where, in_hbm(all_mine), pinned(all_other), pinned(units), in_hbm(proto_weight),
+        in_hbm(all_mine), pinned(all_other), pinned(units), in_hbm(proto_weight),
         pinned(inverse), scale, over_crops(factors), pinned(loss),
     )
     moved = over_crops(grad)

time: 160 us -> 157 us (0.981)
  Pallas kernels: 25.5 us -> 22.7 us
  transfers between devices with their start and end apart: 4 -> 4, of which waited for: 1 -> 1; matrix products, arithmetic and copies ran while one was open for 0% -> 0% of each run, Pallas kernels for 10% -> 9%
where the time goes in v6:
time: 157 us; the launch traced here: 156 us
  blocking collectives  98.7 us (63%)
  Pallas kernels  22.7 us (14%)
  between operations  14.1 us (9%)
  starting transfers between devices  9.96 us (6%)
  waiting for transfers between devices  9.67 us (6%)
    all_to_all x5, blocking collectives, over_crops(): return lax.all_to_all(x, 'crops', 0, 0, tiled=True)  58.2 us
    all_to_all x3, blocking collectives, over_group(): return lax.all_to_all(x, both, 0, 0, tiled=True, axis_index_groups=group)  40.5 us
    all_to_all x1, waiting for transfers between devices, local(): lax.all_to_all(copies, both, 0, 0, tiled=True, axis_index_groups=same_core)  9.63 us
    all_to_all x1, starting transfers between devices, local(): lax.all_to_all(copies, both, 0, 0, tiled=True, axis_index_groups=same_core)  9.55 us
    pallas_call x1, Pallas kernels, local(): pl.pallas_call(functools.partial(grad_kernel, ring), out_shape=(pltpu.VME...  7.46 us
    pallas_call x1, Pallas kernels, local(): pl.pallas_call(last_kernel, out_shape=(struct((protos, 1, 2 * rows + LANE...  3.54 us
  transfers between devices with their start and end apart: 4, of which 1 were waited for; matrix products, arithmetic and copies ran while one was open for 0% of the time, Pallas kernels for 9%

profile of v6, /device:TPU:2, one launch (start us, length us, event | category | flops | bytes accessed | tf_op | source)
XLA Modules:
  0.0 156.1 jit_solution(3881465546515688633)
XLA Ops:
  7.2 1.6 %shard_map.50 = bf16[16,16,768]{2,1,0:T(8,128)(2,1)} custom-call(bf16[16,384]{1,0:T(8,128)(2,1)} %teacher.1, bf16[16,384]{1,0:T(8,128)(2,1)} %student.1), custom_call_target="tpu_custom_call" | custom-call | flops 196608 | bytes 393216 | tf_op jit(solution)/shard_map/pallas_call | solution.py:341
  8.8 9.6 %all-to-all-start = ((bf16[16,16,768]{2,1,0:T(8,128)(2,1)}), bf16[16,16,768]{2,1,0:T(8,128)(2,1)}, u32[]{:S(2)}, u32[]{:S(2)}) async-start(bf16[16,16,768]{2,1,0:T(8,128)(2,1)} %shard_map.50), calls=%async_computation | async-start | bytes 786432 | tf_op jit(solution)/shard_map/all_to_all | solution.py:350
  18.3 0.0 all-gather.2.cloned.1.call-start
  18.4 3.0 %shard_map.51 = (bf16[400,4096]{1,0:T(8,128)(2,1)S(1)}, f32[1,4096]{1,0:T(1,128)S(1)}) custom-call(f32[384,4096]{1,0:T(8,128)} %weight.3), custom_call_target="tpu_custom_call" | custom-call | flops 4718592 | bytes 6291456 | tf_op jit(solution)/shard_map/pallas_call | solution.py:354
  21.4 9.6 %all-to-all-done = bf16[16,16,768]{2,1,0:T(8,128)(2,1)} async-done(((bf16[16,16,768]{2,1,0:T(8,128)(2,1)}), bf16[16,16,768]{2,1,0:T(8,128)(2,1)}, u32[]{:S(2)}, u32[]{:S(2)}) %all-to-all-start) | async-done | bytes 393248 | tf_op jit(solution)/shard_map/all_to_all | solution.py:350
  31.0 0.0 all-gather.2.cloned.1.call-update
  31.0 0.1 collective-permute-start
  31.1 2.2 %shard_map.52 = (f32[512,4096]{1,0:T(8,128)S(1)}, bf16[512,384]{1,0:T(8,128)(2,1)S(1)}, f32[32,128]{1,0:T(8,128)S(1)}) custom-call(bf16[256,768]{1,0:T(8,128)(2,1)} %bitcast.mine, bf16[400,4096]{1,0:T(8,128)(2,1)S(1)} %get-tuple-element.22.units), custom_call_target="tpu_custom_call" | custom-call | flops 805306368 | tf_op jit(solution)/shard_map/pallas_call | solution.py:370
  33.4 0.0 collective-permute-done.other
  33.4 1.3 shard_map.53
  34.6 13.4 %all_to_all.45.parts = f32[8,32,128]{2,1,0:T(8,128)S(1)} all-to-all(f32[8,32,128]{2,1,0:T(8,128)S(1)} %get-tuple-element.27), channel_id=1, replica_groups=mesh['crops'=8,'protos'=32] {'crops'}, dimensions={0} | all-to-all | bytes 262144 | tf_op jit(solution)/shard_map/all_to_all | solution.py:336
  48.0 1.0 shard_map.54
  49.0 14.7 %all_to_all.46.parts = f32[32,4,128]{2,1,0:T(4,128)S(1)} all-to-all(f32[32,4,128]{2,1,0:T(4,128)S(1)} %shard_map.54), channel_id=1, replica_groups={{0,1,2,3,4,5,6,7,8,9,10,11,12,13,14,15,48,49,50,51,52,53,54,55,56,57,58..., dimensions={0} | all-to-all | bytes 131072 | tf_op jit(solution)/shard_map/all_to_all | solution.py:339
  63.6 0.8 shard_map.55
  64.4 10.5 %all_to_all.47.parts = f32[8,32,128]{2,1,0:T(8,128)S(1)} all-to-all(f32[8,32,128]{2,1,0:T(8,128)S(1)} %shard_map.55), channel_id=1, replica_groups=mesh['crops'=8,'protos'=32] {'crops'}, dimensions={0} | all-to-all | bytes 262144 | tf_op jit(solution)/shard_map/all_to_all | solution.py:336
  74.9 1.0 shard_map.56
  75.9 12.0 %all_to_all.48.parts = f32[32,4,128]{2,1,0:T(4,128)S(1)} all-to-all(f32[32,4,128]{2,1,0:T(4,128)S(1)} %shard_map.56), channel_id=1, replica_groups={{0,1,2,3,4,5,6,7,8,9,10,11,12,13,14,15,48,49,50,51,52,53,54,55,56,57,58..., dimensions={0} | all-to-all | bytes 131072 | tf_op jit(solution)/shard_map/all_to_all | solution.py:339
  87.9 0.8 shard_map.57
  88.7 11.0 %all_to_all.49.parts = f32[8,32,128]{2,1,0:T(8,128)S(1)} all-to-all(f32[8,32,128]{2,1,0:T(8,128)S(1)} %shard_map.57), channel_id=1, replica_groups=mesh['crops'=8,'protos'=32] {'crops'}, dimensions={0} | all-to-all | bytes 262144 | tf_op jit(solution)/shard_map/all_to_all | solution.py:336
  99.7 3.5 %shard_map.58 = (f32[32,1,1152]{2,1,0:T(1,128)S(1)}, f32[32,128]{1,0:T(8,128)S(1)}) custom-call(f32[512,4096]{1,0:T(8,128)S(1)} %get-tuple-element.26.table, f32[8,32,128]{2,1,0:T(8,128)S(1)} %all_to_all.49.parts, bf16[512,384]{1,0:T(8,128)(2,1)S(1)} %get-tuple-element.28.student, bf16[400,4096]{1,0:T(8,128)(2,1)S(1)} %get-tuple-element.22.units), custom_call_target="tpu_custom_call" | custom-call | flops 1610612736 | tf_op jit(solution)/shard_map/pallas_call | solution.py:422
  103.3 0.0 all-gather.2.cloned.1.call-done.mine
  103.3 0.3 collective-permute-start.1
  103.6 13.8 %all_to_all.50.parts = f32[32,1,1152]{2,1,0:T(1,128)S(1)} all-to-all(f32[32,1,1152]{2,1,0:T(1,128)S(1)} %get-tuple-element.33), channel_id=1, replica_groups={{0,1,2,3,4,5,6,7,8,9,10,11,12,13,14,15,48,49,50,51,52,53,54,55,56,57,58..., dimensions={0} | all-to-all | bytes 294912 | tf_op jit(solution)/shard_map/all_to_all | solution.py:339
  117.4 0.1 shard_map.59
  117.5 9.7 %all_to_all.51.factors = f32[8,1,1024]{2,1,0:T(1,128)S(1)} all-to-all(f32[8,1,1024]{2,1,0:T(1,128)S(1)} %get-tuple-element.34), channel_id=1, replica_groups=mesh['crops'=8,'protos'=32] {'crops'}, dimensions={0} | all-to-all | bytes 65536 | tf_op jit(solution)/shard_map/all_to_all | solution.py:336
  127.2 0.0 collective-permute-done.1.other
  127.2 7.5 %shard_map.60 = (f32[8,48,512]{2,1,0:T(8,128)S(1)}, f32[1,16]{1,0:T(1,128)}) custom-call(bf16[2048,768]{1,0:T(8,128)(2,1)} %all-gather.2.cloned.1.call-done.mine, bf16[2048,768]{1,0:T(8,128)(2,1)S(1)} %collective-permute-done.1.other, bf16[400,4096]{1,0:T(8,128)(2,1)S(1)} %get-tuple-element.22.units, f32[384,4096]{1,0:T(8,128)} %weight.3, ...), custom_call_target="tpu_custom_call" | custom-call | flops 4831838208 | tf_op jit(solution)/shard_map/pallas_call | solution.py:442
  134.7 13.6 %all_to_all.52 = f32[8,48,512]{2,1,0:T(8,128)S(1)} all-to-all(f32[8,48,512]{2,1,0:T(8,128)S(1)} %get-tuple-element.36), channel_id=1, replica_groups=mesh['crops'=8,'protos'=32] {'crops'}, dimensions={0} | all-to-all | bytes 1572864 | tf_op jit(solution)/shard_map/all_to_all | solution.py:336
  148.3 0.9 copy.8
Async XLA Ops:
  8.8 22.2 %all-to-all-start = ((bf16[16,16,768]{2,1,0:T(8,128)(2,1)}), bf16[16,16,768]{2,1,0:T(8,128)(2,1)}, u32[]{:S(2)}, u32[]{:S(2)}) async-start(bf16[16,16,768]{2,1,0:T(8,128)(2,1)} %shard_map.50), calls=%async_computation | async-start | bytes 786432 | tf_op jit(solution)/shard_map/all_to_all | solution.py:350
  18.3 85.0 %all-gather.2.cloned.1.call-start = ((), (), s32[]{:S(2)}) async-start(), calls=%async_computation.9 | async-start | bytes 3538944 | tf_op jit(solution)/shard_map/all_gather | solution.py:368
  31.0 2.3 %collective-permute-start = (bf16[256,768]{1,0:T(8,128)(2,1)}, bf16[256,768]{1,0:T(8,128)(2,1)S(1)}, u32[]{:S(2)}, u32[]{:S(2)}) collective-permute-start(bf16[256,768]{1,0:T(8,128)(2,1)} %bitcast.mine), channel_id=1, source_target_pairs={{0,1},{1,0},{2,3},{3,2},{4,5},{5,4},{6,7},{7,6},{8,9},{9,8},{10,11... | collective-permute-start | bytes 1179656 | tf_op jit(solution)/shard_map/ppermute | solution.py:367
  103.3 23.9 %collective-permute-start.1 = (bf16[2048,768]{1,0:T(8,128)(2,1)}, bf16[2048,768]{1,0:T(8,128)(2,1)S(1)}, u32[]{:S(2)}, u32[]{:S(2)}) collective-permute-start(bf16[2048,768]{1,0:T(8,128)(2,1)} %all-gather.2.cloned.1.call-done.mine), channel_id=1, source_target_pairs={{0,1},{1,0},{2,3},{3,2},{4,5},{5,4},{6,7},{7,6},{8,9},{9,8},{10,11... | collective-permute-start | bytes 9437192 | tf_op jit(solution)/shard_map/ppermute | solution.py:432
Sparse Core Ops, SparseCore 0:
  31.1 45.1 all-gather.1
